TPU v7x, 256 devices: a whole 4x4x8 slice. The times are simulated.
256 devices in a mesh: section: 16 (over x, z_lo, core), dp: 16 (over y, z_hi).
Axes of the slice: x: 4, y: 4, z: 8 (z_hi: 4, z_lo: 2; z = z_hi * 2 + z_lo), core: 2. Of those that a mesh axis runs over, the one named last changes fastest.
Arguments:
- sent_act: bfloat16 [16, 4096, 4096], P('section', 'dp'), may hold values from -120 to 120
- sent_grad: bfloat16 [16, 4096, 4096], P('section', 'dp'), may hold values from -120 to 120
- embedded: bfloat16 [4096, 4096], P('dp'), may hold values from -120 to 120
- loss_grad: bfloat16 [4096, 4096], P('dp'), may hold values from -120 to 120
- micro_weight: float32 [16, 4], replicated, may hold values from 0.25 to 4
- order: int32 [16, 4], replicated, may hold values from 0 to 3, each once within a row
- assignment: int32 [16, 64], P('section'), may hold values from 0 to 16, as said below
- old_inverse: float32 [16, 64, 128, 128], P('section', 'dp'), may hold values from -3 to 3
Outputs:
- new_inverse: float32 [16, 64, 128, 128], P('section', 'dp')
Inputs may be any that keep to these rules, and one draw needn't show every extreme that they name: assignment[s, b] names the replica that refreshes block b of section s, or is 16 where the block keeps its old inverse; in each section no replica is named more than 8 times, one replica exactly 8 times, and some block keeps its old inverse. `order`: each row is a permutation.
All inputs are finite; a program needn't handle non-finite values.
Results may differ from a plain program's by a relative error of at most 0.0003.
Values may be sent and summed in bfloat16 or wider, within the bound.
A program may use at most 64 MiB of HBM per device.

v0:
```python
import jax
import jax.numpy as jnp
from jax import lax
from jax.sharding import PartitionSpec as P

D = 4096
BLK = 128
MB = 4
MROWS = 64
CAP = 8
NBLK = 64


damping = 0.1


def shifted(block, axis, distance):
    devices = range(lax.axis_size(axis))
    route = [(i - distance, i) for i in devices if i - distance in devices]
    return lax.ppermute(block, axis, route)


def invert_blocks(factor):
    identity = jnp.broadcast_to(jnp.eye(factor.shape[-1], dtype=jnp.float32), factor.shape)
    lower_part = jnp.linalg.cholesky(factor)
    half_solve = lax.linalg.triangular_solve(lower_part, identity, left_side=True, lower=True)
    return lax.linalg.triangular_solve(
        lower_part, half_solve, left_side=True, lower=True, transpose_a=True
    )


def slot_weights(micro_weight, order, section_row, replica):
    ordering = lax.dynamic_index_in_dim(order, section_row, 0, keepdims=False)
    own_weight = lax.dynamic_index_in_dim(micro_weight, replica, 0, keepdims=False)
    batches = jnp.arange(own_weight.shape[0], dtype=jnp.int32)
    return jnp.sum(
        jnp.where(ordering[:, None] == batches[None, :], own_weight[None, :], 0.0), axis=1
    )


def weighted_grams(inputs, weights):
    blocked = inputs.reshape(MB, MROWS, D // BLK, BLK)
    result = jnp.zeros((D // BLK, BLK, BLK), jnp.float32)
    for slot_index in range(MB):
        piece = blocked[slot_index]
        result = result + weights[slot_index] * jnp.einsum(
            "tbi,tbj->bij", piece, piece, preferred_element_type=jnp.float32
        )
    return result


def shards(sent_act, sent_grad, embedded, loss_grad, micro_weight, order, assignment, old_inverse):
    sections = lax.axis_size("section")
    section_at = lax.axis_index("section")
    replica = lax.axis_index("dp")
    replicas = lax.axis_size("dp")
    first_section = section_at == 0
    last_section = section_at == sections - 1
    weight_in = slot_weights(micro_weight, order, jnp.maximum(section_at - 1, 0), replica)
    weight_out = slot_weights(
        micro_weight, order, jnp.minimum(section_at + 1, sections - 1), replica
    )
    own_count = old_inverse.shape[1]
    forward = shifted(sent_act[0], "section", 1)
    backward = shifted(sent_grad[0], "section", -1)
    inputs = jnp.where(first_section, embedded, forward)
    gradients = jnp.where(last_section, loss_grad, backward)
    gram_blocks = jnp.concatenate(
        [weighted_grams(inputs, weight_in), weighted_grams(gradients, weight_out)], axis=0
    )
    reduced = lax.psum(gram_blocks, "dp")
    weight_total = MROWS * jnp.sum(micro_weight)
    identity = jnp.eye(BLK, dtype=jnp.float32)
    assign_row = assignment[0]
    own_assign = lax.dynamic_slice_in_dim(assign_row, replica * own_count, own_count)
    refreshed = own_assign < replicas
    positions = jnp.arange(NBLK, dtype=jnp.int32)
    earlier_same = (assign_row[:, None] == assign_row[None, :]) & (
        positions[None, :] < positions[:, None]
    )
    rank_all = jnp.sum(earlier_same.astype(jnp.int32), axis=1)
    slot_numbers = jnp.arange(CAP, dtype=jnp.int32)
    selector = (
        (assign_row[None, :] == replica) & (rank_all[None, :] == slot_numbers[:, None])
    ).astype(jnp.float32)
    picked = jnp.einsum("cb,bij->cij", selector, reduced, precision=lax.Precision.HIGHEST)
    slot_inverse = invert_blocks(picked / weight_total + damping * identity)
    everyone = lax.all_gather(slot_inverse, "dp", axis=0, tiled=True)
    own_rank = lax.dynamic_slice_in_dim(rank_all, replica * own_count, own_count)
    target = own_assign * CAP + own_rank
    picker = (target[:, None] == jnp.arange(everyone.shape[0], dtype=jnp.int32)[None, :]).astype(
        jnp.float32
    )
    fresh_inverse = jnp.einsum("cs,sij->cij", picker, everyone, precision=lax.Precision.HIGHEST)
    result = jnp.where(refreshed[:, None, None], fresh_inverse, old_inverse[0])
    return result[None]


def solution(mesh):
    in_specs = (
        P("section", "dp", None),
        P("section", "dp", None),
        P("dp", None),
        P("dp", None),
        P(),
        P(),
        P("section", None),
        P("section", "dp", None, None),
    )
    out_specs = P("section", "dp", None, None)
    return jax.shard_map(shards, mesh=mesh, in_specs=in_specs, out_specs=out_specs, check_vma=False)
```

profile of v0, /device:TPU:1, one launch (start us, length us, event | category | flops | bytes accessed | tf_op | source)
XLA Modules:
  0.0 618.4 jit_solution(7269295561453567147)
XLA Ops:
  6.5 4.9 collective-permute-start
  11.5 2.8 collective-permute-start.1
  14.3 0.9 dynamic-slice_reduce_fusion.1
  15.2 1.0 dynamic-slice_reduce_fusion.2
  16.2 0.2 select_reduce_fusion.2
  16.4 0.7 fusion.51
  17.1 17.7 %collective-permute-done = bf16[256,4096]{1,0:T(8,128)(2,1)} collective-permute-done((bf16[256,4096]{1,0:T(8,128)(2,1)}, bf16[256,4096]{1,0:T(8,128)(2,1)}, u32[]{:S(2)}, u32[]{:S(2)}) %collective-permute-start) | collective-permute-done | bytes 2097184 | tf_op jit(solution)/shard_map/ppermute | solution.py:20
  34.7 1.8 broadcast_select_fusion.1
  36.6 0.2 slice_bitcast_fusion.7
  36.7 0.5 fusion.19
  37.2 0.5 fusion.22
  37.7 0.5 fusion.25
  38.2 0.5 fusion.28
  38.7 19.6 %collective-permute-done.1 = bf16[256,4096]{1,0:T(8,128)(2,1)S(1)} collective-permute-done((bf16[256,4096]{1,0:T(8,128)(2,1)}, bf16[256,4096]{1,0:T(8,128)(2,1)S(1)}, u32[]{:S(2)}, u32[]{:S(2)}) %collective-permute-start.1) | collective-permute-done | bytes 2097184 | tf_op jit(solution)/shard_map/ppermute | solution.py:20
  58.3 0.3 broadcast_select_fusion
  58.6 0.2 slice_bitcast_fusion.3
  58.8 0.5 fusion.10
  59.3 0.5 fusion.13
  59.7 0.5 fusion.16
  60.2 0.5 fusion.7
  60.7 6.9 %fusion.3 = f32[32,128,128]{2,0,1:T(8,128)S(1)} fusion(f32[32,128,128]{2,1,0:T(8,128)S(1)} %fusion.19, f32[32,128,128]{2,1,0:T(8,128)S(1)} %fusion.22, f32[32,128,128]{2,1,0:T(8,128)S(1)} %fusion.25, f32[32,128,128]{2,1,0:T(8,128)S(1)} %fusion.28, f32[]{:T(128)} %bitcast.10, f32[]{:T(128)} %bitcast.9, f32[]{:T(128)} %bitcast.8, f32[]{:T(128)} %bitcast.6), kind=kLoop, calls=%fused_computation.9 | loop fusion | flops 3670016 | bytes 10485776 | tf_op jit(solution)/shard_map/add | solution.py:46
  67.7 7.0 %fusion = f32[32,128,128]{2,0,1:T(8,128)S(1)} fusion(f32[32,128,128]{2,1,0:T(8,128)S(1)} %fusion.7, f32[32,128,128]{2,1,0:T(8,128)S(1)} %fusion.10, f32[32,128,128]{2,1,0:T(8,128)S(1)} %fusion.13, f32[32,128,128]{2,1,0:T(8,128)S(1)} %fusion.16, f32[]{:T(128)} %bitcast.15, f32[]{:T(128)} %bitcast.14, f32[]{:T(128)} %bitcast.13, f32[]{:T(128)} %bitcast.11), kind=kLoop, calls=%fused_computation.2 | loop fusion | flops 3670016 | bytes 10485776 | tf_op jit(solution)/shard_map/add | solution.py:46
  74.7 2.4 pad_maximum_fusion
  77.1 0.0 all-gather.2.cloned.1.call-start
  77.1 0.6 copy-done.2
  77.7 0.6 reduce_sum.39
  78.3 0.1 copy.15
  79.2 0.2 convert_reduce_fusion
  79.4 217.1 %all-reduce.2.cloned.1.call-done = f32[64,128,128]{2,0,1:T(8,128)} async-done(((f32[64,128,128]{2,0,1:T(8,128)}), f32[64,128,128]{2,0,1:T(8,128)}) %all-reduce.2.cloned.1.call-update) | async-done | bytes 4194320 | tf_op jit(solution)/shard_map/psum | solution.py:71
  296.5 3.7 fusion.44
  300.2 0.2 copy.14
  300.4 0.1 broadcast_add_fusion
  300.4 0.2 copy.16
  300.7 0.1 fusion.36
  300.8 93.8 %custom-call.9 = f32[8,128,128]{2,1,0:T(8,128)S(1)} custom-call(f32[8,128,128]{2,1,0:T(8,128)S(1)} %fusion.36), custom_call_target="Cholesky" | custom-call | tf_op jit(solution)/shard_map/jit(cholesky)/cholesky | solution.py:25
  394.5 0.1 select_reduce_fusion
  394.6 0.1 compare_reduce_fusion
  394.7 0.1 select_bitcast_fusion
  394.8 78.6 %custom-call.10 = f32[8,1,128,128]{2,3,1,0:T(8,128)S(1)} custom-call(f32[8,1,128,128]{3,2,1,0:T(8,128)S(1)} %select_bitcast_fusion), custom_call_target="InvertDiagBlocksLowerTriangular" | custom-call | tf_op jit(solution)/shard_map/triangular_solve | solution.py:27
  473.5 1.0 fusion.33
  474.5 0.7 fusion.31
  475.1 1.2 copy.35
  476.3 0.0 all-gather.2.cloned.1.call-update
  476.3 0.1 bitcast_add_fusion.1
  476.4 0.1 compare_bitcast_fusion.1
  476.5 128.2 %all-gather.2.cloned.1.call-done = f32[128,128,128]{2,0,1:T(8,128)} async-done(((f32[8,128,128]{2,0,1:T(8,128)}), f32[128,128,128]{2,0,1:T(8,128)}) %all-gather.2.cloned.1.call-update) | async-done | bytes 8388624 | tf_op jit(solution)/shard_map/all_gather | solution.py:88
  604.7 6.2 %fusion.6 = f32[1,4,128,128]{3,1,2,0:T(4,128)S(1)} fusion(f32[128,128,128]{2,0,1:T(8,128)} %all-gather.2.cloned.1.call-done, f32[1,4,128,128]{3,2,1,0:T(8,128)S(1)} %copy-done.1, pred[4]{0:T(512)(128)(4,1)S(1)} %compare_bitcast_fusion.1, s32[4]{0:T(128)S(1)} %bitcast_add_fusion.1), kind=kOutput, calls=%fused_computation.18 | convolution fusion | flops 100729344 | bytes 8912916 | tf_op jit(solution)/shard_map/cs,sij->cij/dot_general | solution.py:94
  610.9 0.7 copy.18
  (15 shorter events, 0.1 us)
Async XLA Ops:
  6.5 290.0 %all-reduce.2.cloned.1.call-start = ((), (), s32[]{:S(2)}) async-start(), calls=%async_computation | async-start | bytes 8388608 | tf_op jit(solution)/shard_map/psum | solution.py:71
  6.5 28.2 %collective-permute-start = (bf16[256,4096]{1,0:T(8,128)(2,1)}, bf16[256,4096]{1,0:T(8,128)(2,1)}, u32[]{:S(2)}, u32[]{:S(2)}) collective-permute-start(bf16[256,4096]{1,0:T(8,128)(2,1)} %bitcast.84), channel_id=1, source_target_pairs={{0,16},{16,32},{32,48},{48,64},{64,80},{80,96},{96,112},{112,128},... | collective-permute-start | bytes 6291464 | tf_op jit(solution)/shard_map/ppermute | solution.py:20
  11.5 46.8 %collective-permute-start.1 = (bf16[256,4096]{1,0:T(8,128)(2,1)}, bf16[256,4096]{1,0:T(8,128)(2,1)S(1)}, u32[]{:S(2)}, u32[]{:S(2)}) collective-permute-start(bf16[256,4096]{1,0:T(8,128)(2,1)} %bitcast.85), channel_id=1, source_target_pairs={{16,0},{32,16},{48,32},{64,48},{80,64},{96,80},{112,96},{128,112},... | collective-permute-start | bytes 6291464 | tf_op jit(solution)/shard_map/ppermute | solution.py:20
  37.7 20.6 %copy-start = (bf16[256,4096]{1,0:T(8,128)(2,1)S(1)}, bf16[256,4096]{1,0:T(8,128)(2,1)}, u32[]{:S(2)}) copy-start(bf16[256,4096]{1,0:T(8,128)(2,1)} %param.11) | copy-start | bytes 6291460
  77.0 0.7 copy-start.2
  77.0 2.1 copy-start.3
  77.1 527.6 %all-gather.2.cloned.1.call-start = ((), (), s32[]{:S(2)}) async-start(), calls=%async_computation.1 | async-start | bytes 8912896 | tf_op jit(solution)/shard_map/all_gather | solution.py:88
  473.4 131.2 %copy-start.1 = (f32[1,4,128,128]{3,2,1,0:T(8,128)S(1)}, f32[1,4,128,128]{3,2,1,0:T(8,128)}, u32[]{:S(2)}) copy-start(f32[1,4,128,128]{3,2,1,0:T(8,128)} %param.15) | copy-start | bytes 786436
Sparse Core Ops, SparseCore 0:
  77.2 219.2 all-reduce.1
  476.4 128.1 all-gather.1
where the time goes:
time: 619 us; the launch traced here: 618 us
  waiting for transfers between devices  383 us (62%)
  other arithmetic  192 us (31%)
  matrix products  15.4 us (2%)
  between operations  14.3 us (2%)
  starting transfers between devices  7.81 us (1%)
    psum x1, waiting for transfers between devices, shards(): reduced = lax.psum(gram_blocks, 'dp')  217 us
    all_gather x1, waiting for transfers between devices, shards(): everyone = lax.all_gather(slot_inverse, 'dp', axis=0, tiled=True)  128 us
    another operation x4, other arithmetic, invert_blocks(): lower_part = jnp.linalg.cholesky(factor)  94 us
    another operation x3, other arithmetic, invert_blocks(): lax.linalg.triangular_solve(lower_part, half_solve, left_side=True, lower...  78.7 us
    ppermute x2, waiting for transfers between devices, shifted(): return lax.ppermute(block, axis, route)  37.3 us
    add x2, other arithmetic, weighted_grams(): result + weights[slot_index] * jnp.einsum('tbi,tbj->bij', piece, piece, p...  13.9 us
  transfers between devices with their start and end apart: 4, of which 4 were waited for; matrix products, arithmetic and copies ran while one was open for 1% of the time, Pallas kernels for 0%

commit v1 on v0

v1 whole, which is shorter than its diff:
```python
import jax
import jax.numpy as jnp
from jax import lax
from jax.experimental import pallas as pl
from jax.experimental.pallas import tpu as pltpu
from jax.sharding import PartitionSpec as P

D = 4096
BLK = 128
MB = 4
MROWS = 64
ROWS = MB * MROWS
NBLK = 64
OWN = 4
SIDE = 4
SECTIONS = 16
REPLICAS = 16
PACKED = BLK + 8
PANEL = 8
MESH = pl.DeviceIdType.MESH

damping = 0.1


def flip1(v):
    return v + 1 - 2 * (v % 2)


def flip2(v):
    return (v + 2) % 4


def flip3(v):
    return 3 - v


def spread(v, half):
    if half == 0:
        return flip2(v), flip1(v), flip3(v), v
    return flip2(v), flip3(v), flip1(v), v


def final_target(s, y):
    low, last, inner = 1 - y // 2, s // (SECTIONS - 1), (s + SECTIONS - 1) // SECTIONS
    to_s = s + low * (1 - last) - (1 - low) * inner
    to_y = y + 2 * low * last - 2 * (1 - low) * (1 - inner)
    return to_s, to_y


def final_source(s, y):
    low, last, inner = 1 - y // 2, s // (SECTIONS - 1), (s + SECTIONS - 1) // SECTIONS
    from_s = s - low * inner + (1 - low) * (1 - last)
    from_y = y + 2 * low * (1 - inner) - 2 * (1 - low) * last
    return from_s, from_y


def reduce_kernel(
    sent_act, sent_grad, embedded, loss_grad, micro_weight, order, out,
    rows, acc, got_y1, got_y2, got_z1, got_f, in_sem,
    y1_send, y1_recv, y2_send, y2_recv, z1_send, z1_recv, f_send, f_recv,
):
    s = lax.axis_index("section")
    r = lax.axis_index("dp")
    y, z = r // SIDE, r % SIDE

    def fetch(src, part):
        return pltpu.make_async_copy(src, rows.at[:, pl.ds(part * D, D)], in_sem.at[part])

    @pl.when(s < SECTIONS - 1)
    def _():
        fetch(sent_act.at[0], 0).start()

    @pl.when(s == SECTIONS - 1)
    def _():
        fetch(loss_grad, 0).start()

    @pl.when(s > 0)
    def _():
        fetch(sent_grad.at[0], 1).start()

    @pl.when(s == 0)
    def _():
        fetch(embedded, 1).start()

    barrier = pltpu.get_barrier_semaphore()
    from_s, from_y = final_source(s, y)
    greet = [(s, flip1(y), z), (s, flip3(y), z), (s, y, flip1(z)), (s, y, flip3(z))]
    greet += [(from_s, from_y, z), (from_s, from_y, flip1(z)), (from_s, from_y, flip3(z))]
    for to_s, to_y, to_z in greet:
        pl.semaphore_signal(
            barrier, inc=1, device_id=(to_s, to_y * SIDE + to_z), device_id_type=MESH
        )

    weights = []
    for slot in range(MB):
        batch = order[s, slot]
        weight = jnp.float32(0.0)
        for m in range(MB):
            weight = weight + jnp.where(batch == m, micro_weight[r, m], 0.0)
        weights.append(weight)

    row_at = lax.broadcasted_iota(jnp.int32, (BLK, BLK), 0)
    col_at = lax.broadcasted_iota(jnp.int32, (BLK, BLK), 1)

    def gram(first_column):
        total = None
        for slot in range(MB):
            piece = rows[slot * MROWS:(slot + 1) * MROWS,
                         pl.ds(pl.multiple_of(first_column, BLK), BLK)]
            term = lax.dot_general(
                piece, piece, (((0,), (0,)), ((), ())), preferred_element_type=jnp.float32
            )
            term = weights[slot] * term
            total = term if total is None else total + term
        return total

    def compute(chunk, first_y_slot):
        for half in range(2):
            y_order, z_order = spread(y, half), spread(z, half)

            def body(i, carry):
                z_slot = i % 2
                y_at = jnp.where(i // 2 == 0, y_order[first_y_slot], y_order[first_y_slot + 1])
                z_at = jnp.where(z_slot == 0, z_order[2 * chunk], z_order[2 * chunk + 1])
                column = ((y_at * SIDE + z_at) * OWN + 2 * half) * BLK
                one, two = gram(column), gram(column + BLK)
                place = acc.at[half, chunk, first_y_slot + i // 2, z_slot]
                place[:BLK, :] = jnp.where(row_at >= col_at, one, two)
                diagonal = jnp.sum(
                    jnp.where(row_at == col_at, two, 0.0), axis=0, keepdims=True
                )
                place[BLK:, :] = jnp.broadcast_to(diagonal, (8, BLK))
                return carry

            lax.fori_loop(0, 4, body, 0)

    def remote(src, dst, send, recv, to):
        return pltpu.make_async_remote_copy(
            src_ref=src, dst_ref=dst, send_sem=send, recv_sem=recv,
            device_id=(to[0], to[1] * SIDE + to[2]), device_id_type=MESH,
        )

    y_first = [flip1(y), flip3(y)]
    y_second = [flip3(y), flip1(y)]
    z_first = [flip1(z), flip3(z)]
    z_second = [flip3(z), flip1(z)]
    to_s, to_y = final_target(s, y)

    step_y1 = [[remote(acc.at[h, c, pl.ds(0, 2)], got_y1.at[h, c], y1_send.at[h, c],
                       y1_recv.at[h, c], (s, y_first[h], z)) for c in range(2)] for h in range(2)]
    step_y2 = [[remote(acc.at[h, c, 2], got_y2.at[h, c], y2_send.at[h, c],
                       y2_recv.at[h, c], (s, y_second[h], z)) for c in range(2)] for h in range(2)]
    step_z1 = [remote(acc.at[h, 0, 3], got_z1.at[h], z1_send.at[h], z1_recv.at[h],
                      (s, y, z_first[h])) for h in range(2)]
    step_f = [[remote(acc.at[h, 1, 3, 0], got_f.at[h, 0], f_send.at[h, 0], f_recv.at[h, 0],
                      (to_s, to_y, z_second[h])),
               remote(acc.at[h, 1, 3, 1], got_f.at[h, 1], f_send.at[h, 1], f_recv.at[h, 1],
                      (to_s, to_y, z))] for h in range(2)]

    for part in range(2):
        fetch(sent_act.at[0], part).wait()
    compute(0, 0)
    pl.semaphore_wait(barrier, len(greet))
    for h in range(2):
        step_y1[h][0].start()
    compute(1, 0)
    for h in range(2):
        step_y1[h][1].start()
    compute(0, 2)
    compute(1, 2)

    for c in range(2):
        for h in range(2):
            step_y1[h][c].wait_recv()
            acc[h, c, 2] = acc[h, c, 2] + got_y1[h, c, 0]
            step_y2[h][c].start()
            acc[h, c, 3] = acc[h, c, 3] + got_y1[h, c, 1]
    for h in range(2):
        step_y2[h][0].wait_recv()
        acc[h, 0, 3] = acc[h, 0, 3] + got_y2[h, 0]
        step_z1[h].start()
    for h in range(2):
        step_y2[h][1].wait_recv()
        acc[h, 1, 3] = acc[h, 1, 3] + got_y2[h, 1]
    for h in range(2):
        step_z1[h].wait_recv()
        for i in range(2):
            acc[h, 1, 3, i] = acc[h, 1, 3, i] + got_z1[h, i]
            step_f[h][i].start()
    for h in range(2):
        for c in range(2):
            step_y1[h][c].wait_send()
            step_y2[h][c].wait_send()
        step_z1[h].wait_send()
    for h in range(2):
        for i in range(2):
            step_f[h][i].wait_recv()
        out[h] = got_f[h, 0] + got_f[h, 1]
    for h in range(2):
        for i in range(2):
            step_f[h][i].wait_send()


def reduce_blocks(sent_act, sent_grad, embedded, loss_grad, micro_weight, order):
    dma = pltpu.SemaphoreType.DMA
    block = (PACKED, BLK)
    hbm, smem = pl.BlockSpec(memory_space=pl.ANY), pl.BlockSpec(memory_space=pltpu.SMEM)
    return pl.pallas_call(
        reduce_kernel,
        out_shape=jax.ShapeDtypeStruct((2,) + block, jnp.float32),
        in_specs=[hbm] * 4 + [smem] * 2,
        out_specs=pl.BlockSpec(memory_space=pltpu.VMEM),
        scratch_shapes=[
            pltpu.VMEM((ROWS, 2 * D), jnp.bfloat16),
            pltpu.VMEM((2, 2, 4, 2) + block, jnp.float32),
            pltpu.VMEM((2, 2, 2, 2) + block, jnp.float32),
            pltpu.VMEM((2, 2, 2) + block, jnp.float32),
            pltpu.VMEM((2, 2) + block, jnp.float32),
            pltpu.VMEM((2, 2) + block, jnp.float32),
            dma((2,)),
            dma((2, 2)), dma((2, 2)), dma((2, 2)), dma((2, 2)),
            dma((2,)), dma((2,)), dma((2, 2)), dma((2, 2)),
        ],
        compiler_params=pltpu.CompilerParams(
            collective_id=0, has_side_effects=True, vmem_limit_bytes=32 * 1024 * 1024
        ),
        name="gram_reduce",
    )(sent_act, sent_grad, embedded, loss_grad, micro_weight, order)


def split3(x):
    high = x.astype(jnp.bfloat16)
    rest = x - high.astype(jnp.float32)
    middle = rest.astype(jnp.bfloat16)
    low = (rest - middle.astype(jnp.float32)).astype(jnp.bfloat16)
    return high, middle, low


def invert_kernel(micro_weight, assignment, packed, old, out, work):
    r = lax.axis_index("dp")
    row_at = lax.broadcasted_iota(jnp.int32, (BLK, BLK), 0)
    col_at = lax.broadcasted_iota(jnp.int32, (BLK, BLK), 1)
    weight_sum = jnp.sum(
        jnp.sum(micro_weight[...], axis=1, keepdims=True), axis=0, keepdims=True
    )
    scale = 1.0 / (MROWS * weight_sum)
    shift = jnp.where(row_at == col_at, jnp.float32(damping), 0.0)
    for half in range(2):
        square = packed[half, :BLK, :]
        flipped = square.T
        one = jnp.where(row_at >= col_at, square, flipped)
        two = jnp.where(row_at < col_at, square, flipped)
        two = jnp.where(row_at == col_at, packed[half, BLK:BLK + 1, :], two)
        work[2 * half] = one * scale + shift
        work[2 * half + 1] = two * scale + shift

    sub = lax.broadcasted_iota(jnp.int32, (PANEL, BLK), 0)
    lane = lax.broadcasted_iota(jnp.int32, (PANEL, BLK), 1)

    def spread_row(x, k):
        return jnp.broadcast_to(x[k:k + 1, :], (PANEL, BLK))

    for p in range(BLK // PANEL):
        start = p * PANEL
        inside = (lane >= start) & (lane < start + PANEL)
        panel_cols = (col_at >= start) & (col_at < start + PANEL)
        original = [work[m, start:start + PANEL, :] for m in range(OWN)]
        state = list(original)
        columns = [
            [jnp.broadcast_to(x[:, start + j:start + j + 1], (PANEL, BLK)) for j in range(PANEL)]
            for x in original
        ]
        for k in range(PANEL):
            for m in range(OWN):
                here = columns[m][k]
                inverse = 1.0 / spread_row(here, k)
                marked = jnp.where(lane == start + k, jnp.where(sub == k, 1.0, 0.0), state[m])
                pivot_row = spread_row(marked, k) * inverse
                state[m] = jnp.where(sub == k, pivot_row, marked - here * pivot_row)
                for j in range(k + 1, PANEL):
                    step = spread_row(columns[m][j], k) * inverse
                    columns[m][j] = jnp.where(sub == k, step, columns[m][j] - here * step)
        for m in range(OWN):
            swept = jnp.where(inside, -state[m], state[m])
            h0, m0, l0 = split3(original[m])
            h1, m1, l1 = split3(swept)
            left = jnp.concatenate([h0, h0, m0, m0, h0, l0], axis=0)
            right = jnp.concatenate([h1, m1, h1, m1, l1, h1], axis=0)
            update = lax.dot_general(
                left, right, (((0,), (0,)), ((), ())), preferred_element_type=jnp.float32
            )
            work[m] = jnp.where(panel_cols, 0.0, work[m]) - update
            work[m, start:start + PANEL, :] = swept

    for m in range(OWN):
        refreshed = assignment[0, r * OWN + m] < REPLICAS
        out[0, m] = jnp.where(refreshed, -work[m], old[0, m])


def invert_blocks(micro_weight, assignment, packed, old_inverse):
    vmem, smem = pl.BlockSpec(memory_space=pltpu.VMEM), pl.BlockSpec(memory_space=pltpu.SMEM)
    return pl.pallas_call(
        invert_kernel,
        out_shape=jax.ShapeDtypeStruct(old_inverse.shape, jnp.float32),
        in_specs=[vmem, smem, vmem, vmem],
        out_specs=vmem,
        scratch_shapes=[pltpu.VMEM((OWN, BLK, BLK), jnp.float32)],
        compiler_params=pltpu.CompilerParams(vmem_limit_bytes=32 * 1024 * 1024),
        name="invert",
    )(micro_weight, assignment, packed, old_inverse)


def shards(sent_act, sent_grad, embedded, loss_grad, micro_weight, order, assignment, old_inverse):
    packed = reduce_blocks(sent_act, sent_grad, embedded, loss_grad, micro_weight, order)
    return invert_blocks(micro_weight, assignment, packed, old_inverse)


def solution(mesh):
    in_specs = (
        P("section", "dp", None),
        P("section", "dp", None),
        P("dp", None),
        P("dp", None),
        P(),
        P(),
        P("section", None),
        P("section", "dp", None, None),
    )
    out_specs = P("section", "dp", None, None)
    return jax.shard_map(shards, mesh=mesh, in_specs=in_specs, out_specs=out_specs, check_vma=False)
```

time: 619 us -> 57.6 us (0.09)
  waiting for transfers between devices: 383 us -> 0 us
  other arithmetic: 192 us -> 0 us
  Pallas kernels: 0 us -> 49.4 us
  matrix products: 15.4 us -> 0 us
  between operations: 14.3 us -> 0.03 us
  starting transfers between devices: 7.81 us -> 0 us
    psum x1 -> x0, waiting for transfers between devices: 217 us -> none  [shards(): reduced = lax.psum(gram_blocks, 'dp')]
    another operation x7 -> x0, other arithmetic: 173 us -> none  [the longest x4 94 us: invert_blocks(): lower_part = jnp.linalg.cholesky(factor)]
    all_gather x1 -> x0, waiting for transfers between devices: 128 us -> none  [shards(): everyone = lax.all_gather(slot_inverse, 'dp', axis=0, tiled=True)]
    pallas_call x0 -> x2, Pallas kernels: none -> 49.4 us  [the longest x1 41.9 us: reduce_blocks(): pl.pallas_call(reduce_kernel, out_shape=jax.ShapeDtypeStruct((2,) + block...]
    ppermute x2 -> x0, waiting for transfers between devices: 37.3 us -> none  [shifted(): return lax.ppermute(block, axis, route)]
    add x4 -> x0, other arithmetic: 14 us -> none  [the longest x2 13.9 us: weighted_grams(): result + weights[slot_index] * jnp.einsum('tbi,tbj->bij', piece, piece, p...]
    dot_general x10 -> x0, matrix products: 13.8 us -> none  [the longest x1 6.19 us: shards(): jnp.einsum('cs,sij->cij', picker, everyone, precision=lax.Precision.HIGHEST)]
    ppermute x2 -> x0, starting transfers between devices: 7.77 us -> none  [shifted(): return lax.ppermute(block, axis, route)]
  transfers between devices with their start and end apart: 4 -> 0, of which waited for: 4 -> 0; matrix products, arithmetic and copies ran while one was open for 1% -> 0% of each run, Pallas kernels for 0% -> 0%
where the time goes in v1:
time: 57.6 us; the launch traced here: 57.3 us
  Pallas kernels  49.4 us (86%)
  local copies, waits for them, and re-layouts  7.88 us (14%)
    pallas_call x1, Pallas kernels, reduce_blocks(): pl.pallas_call(reduce_kernel, out_shape=jax.ShapeDtypeStruct((2,) + block...  41.9 us
    unnamed x14, local copies, waits for them, and re-layouts  7.88 us
    pallas_call x1, Pallas kernels, invert_blocks(): pl.pallas_call(invert_kernel, out_shape=jax.ShapeDtypeStruct(old_inverse....  7.54 us

profile of v1, /device:TPU:1, one launch (start us, length us, event | category | flops | bytes accessed | tf_op | source)
XLA Modules:
  0.0 57.3 jit_solution(16505340145585978982)
XLA Ops:
  0.0 0.8 %copy.11.micro_weight = f32[16,4]{1,0:T(8,128)S(1)} copy(f32[16,4]{0,1:T(4,128)} %param.12) | data formatting | bytes 512 | tf_op args[4]
  0.8 0.8 %copy.10.order = s32[16,4]{1,0:T(8,128)S(1)} copy(s32[16,4]{0,1:T(4,128)} %param.13) | data formatting | bytes 512 | tf_op args[5]
  1.5 0.0 copy-start
  1.5 1.6 %copy-done = bf16[1,256,4096]{2,1,0:T(8,128)(2,1)S(1)} copy-done((bf16[1,256,4096]{2,1,0:T(8,128)(2,1)S(1)}, bf16[1,256,4096]{2,1,0:T(8,128)(2,1)}, u32[]{:S(2)}) %copy-start) | copy-done | bytes 2097176
  3.1 0.0 copy-start.1
  3.1 1.6 %copy-done.1 = bf16[1,256,4096]{2,1,0:T(8,128)(2,1)S(1)} copy-done((bf16[1,256,4096]{2,1,0:T(8,128)(2,1)S(1)}, bf16[1,256,4096]{2,1,0:T(8,128)(2,1)}, u32[]{:S(2)}) %copy-start.1) | copy-done | bytes 2097176
  4.7 0.0 copy-start.2
  4.7 1.6 %copy-done.2 = bf16[256,4096]{1,0:T(8,128)(2,1)S(1)} copy-done((bf16[256,4096]{1,0:T(8,128)(2,1)S(1)}, bf16[256,4096]{1,0:T(8,128)(2,1)}, u32[]{:S(2)}) %copy-start.2) | copy-done | bytes 2097176
  6.3 0.0 copy-start.3
  6.3 1.6 %copy-done.3 = bf16[256,4096]{1,0:T(8,128)(2,1)S(1)} copy-done((bf16[256,4096]{1,0:T(8,128)(2,1)S(1)}, bf16[256,4096]{1,0:T(8,128)(2,1)}, u32[]{:S(2)}) %copy-start.3) | copy-done | bytes 2097176
  7.9 0.0 copy-start.4
  7.9 0.0 copy-start.5
  7.9 41.9 %gram_reduce.1.packed = f32[2,136,128]{2,1,0:T(8,128)S(1)} custom-call(bf16[1,256,4096]{2,1,0:T(8,128)(2,1)S(1)} %copy-done, bf16[1,256,4096]{2,1,0:T(8,128)(2,1)S(1)} %copy-done.1, bf16[256,4096]{1,0:T(8,128)(2,1)S(1)} %copy-done.2, bf16[256,4096]{1,0:T(8,128)(2,1)S(1)} %copy-done.3, f32[16,4]{1,0:T(8,128)S(1)} %copy.11.micro_weight, s32[16,4]{1,0:T(8,128)S(1)} %copy.10.order), custom_call_target="tpu_custom_call" | custom-call | tf_op jit(solution)/shard_map/gram_reduce/pallas_call | solution.py:208
  49.8 0.0 copy-done.4
  49.8 0.0 copy-done.5
  49.8 7.5 %invert.1 = f32[1,4,128,128]{3,2,1,0:T(8,128)} custom-call(f32[16,4]{1,0:T(8,128)S(1)} %copy.11.micro_weight, s32[1,64]{1,0:T(1,128)S(1)} %copy-done.5, f32[2,136,128]{2,1,0:T(8,128)S(1)} %gram_reduce.1.packed, f32[1,4,128,128]{3,2,1,0:T(8,128)S(1)} %copy-done.4), custom_call_target="tpu_custom_call" | custom-call | tf_op jit(solution)/shard_map/invert/pallas_call | solution.py:302
Async XLA Ops:
  1.5 1.6 %copy-start = (bf16[1,256,4096]{2,1,0:T(8,128)(2,1)S(1)}, bf16[1,256,4096]{2,1,0:T(8,128)(2,1)}, u32[]{:S(2)}) copy-start(bf16[1,256,4096]{2,1,0:T(8,128)(2,1)} %sent_act.1) | copy-start | bytes 6291460
  3.1 1.6 %copy-start.1 = (bf16[1,256,4096]{2,1,0:T(8,128)(2,1)S(1)}, bf16[1,256,4096]{2,1,0:T(8,128)(2,1)}, u32[]{:S(2)}) copy-start(bf16[1,256,4096]{2,1,0:T(8,128)(2,1)} %sent_grad.1) | copy-start | bytes 6291460
  4.7 1.6 %copy-start.2 = (bf16[256,4096]{1,0:T(8,128)(2,1)S(1)}, bf16[256,4096]{1,0:T(8,128)(2,1)}, u32[]{:S(2)}) copy-start(bf16[256,4096]{1,0:T(8,128)(2,1)} %embedded.1) | copy-start | bytes 6291460
  6.3 1.6 %copy-start.3 = (bf16[256,4096]{1,0:T(8,128)(2,1)S(1)}, bf16[256,4096]{1,0:T(8,128)(2,1)}, u32[]{:S(2)}) copy-start(bf16[256,4096]{1,0:T(8,128)(2,1)} %loss_grad.1) | copy-start | bytes 6291460
  7.9 41.9 %copy-start.4 = (f32[1,4,128,128]{3,2,1,0:T(8,128)S(1)}, f32[1,4,128,128]{3,2,1,0:T(8,128)}, u32[]{:S(2)}) copy-start(f32[1,4,128,128]{3,2,1,0:T(8,128)} %old.1) | copy-start | bytes 786436
  7.9 41.9 %copy-start.5 = (s32[1,64]{1,0:T(1,128)S(1)}, s32[1,64]{1,0:T(1,128)}, u32[]{:S(2)}) copy-start(s32[1,64]{1,0:T(1,128)} %assignment.1) | copy-start | bytes 772

commit v2 on v1

--- a/solution.py
+++ b/solution.py
@@ -17,6 +17,7 @@
 REPLICAS = 16
 PACKED = BLK + 8
 PANEL = 8
+VMEM_LIMIT = 60 * 1024 * 1024
 MESH = pl.DeviceIdType.MESH
 
 damping = 0.1
@@ -56,31 +57,46 @@
 
 def reduce_kernel(
     sent_act, sent_grad, embedded, loss_grad, micro_weight, order, out,
-    rows, acc, got_y1, got_y2, got_z1, got_f, in_sem,
+    rows, give, keep, got_y1, got_y2, got_z1, got_f, in_sem,
     y1_send, y1_recv, y2_send, y2_recv, z1_send, z1_recv, f_send, f_recv,
 ):
     s = lax.axis_index("section")
     r = lax.axis_index("dp")
     y, z = r // SIDE, r % SIDE
-
-    def fetch(src, part):
-        return pltpu.make_async_copy(src, rows.at[:, pl.ds(part * D, D)], in_sem.at[part])
-
-    @pl.when(s < SECTIONS - 1)
-    def _():
-        fetch(sent_act.at[0], 0).start()
-
-    @pl.when(s == SECTIONS - 1)
-    def _():
-        fetch(loss_grad, 0).start()
-
-    @pl.when(s > 0)
-    def _():
-        fetch(sent_grad.at[0], 1).start()
-
-    @pl.when(s == 0)
-    def _():
-        fetch(embedded, 1).start()
+    fetch_order = (flip2(z), flip1(z), flip3(z), z)
+
+    def fetch(src, to_y, place):
+        column = (to_y * SIDE + fetch_order[place]) * OWN * BLK
+        wide = pl.ds(pl.multiple_of(column, OWN * BLK), OWN * BLK)
+        narrow = pl.ds(pl.multiple_of(column - to_y // 2 * D, OWN * BLK), OWN * BLK)
+        return pltpu.make_async_copy(
+            src.at[:, narrow], rows.at[:, wide], in_sem.at[place, to_y]
+        )
+
+    for place in range(SIDE):
+        @pl.when(s < SECTIONS - 1)
+        def _():
+            for to_y in range(2):
+                fetch(sent_act.at[0], to_y, place).start()
+
+        @pl.when(s == SECTIONS - 1)
+        def _():
+            for to_y in range(2):
+                fetch(loss_grad, to_y, place).start()
+
+        @pl.when(s > 0)
+        def _():
+            for to_y in range(2, 4):
+                fetch(sent_grad.at[0], to_y, place).start()
+
+        @pl.when(s == 0)
+        def _():
+            for to_y in range(2, 4):
+                fetch(embedded, to_y, place).start()
+
+    def fetched(place):
+        for to_y in range(SIDE):
+            fetch(sent_act.at[0], to_y, place).wait()
 
     barrier = pltpu.get_barrier_semaphore()
     from_s, from_y = final_source(s, y)
@@ -93,46 +109,54 @@
 
     weights = []
     for slot in range(MB):
-        batch = order[s, slot]
+        batch = order[slot, s]
         weight = jnp.float32(0.0)
         for m in range(MB):
-            weight = weight + jnp.where(batch == m, micro_weight[r, m], 0.0)
+            weight = weight + jnp.where(batch == m, micro_weight[m, r], 0.0)
         weights.append(weight)
 
     row_at = lax.broadcasted_iota(jnp.int32, (BLK, BLK), 0)
     col_at = lax.broadcasted_iota(jnp.int32, (BLK, BLK), 1)
-
-    def gram(first_column):
+    blank = jnp.zeros((MROWS, BLK), jnp.bfloat16)
+    y_orders, z_orders = [spread(y, h) for h in range(2)], [spread(z, h) for h in range(2)]
+
+    def unit(half, y_at, z_at):
+        column = ((y_at * SIDE + z_at) * OWN + 2 * half) * BLK
         total = None
         for slot in range(MB):
-            piece = rows[slot * MROWS:(slot + 1) * MROWS,
-                         pl.ds(pl.multiple_of(first_column, BLK), BLK)]
-            term = lax.dot_general(
-                piece, piece, (((0,), (0,)), ((), ())), preferred_element_type=jnp.float32
+            at = pl.ds(slot * MROWS, MROWS)
+            one = rows[at, pl.ds(pl.multiple_of(column, 2 * BLK), BLK)]
+            two = rows[at, pl.ds(pl.multiple_of(column + BLK, BLK), BLK)]
+            left = jnp.concatenate([one, two], axis=0)
+            right = jnp.concatenate(
+                [jnp.concatenate([one, blank], axis=1), jnp.concatenate([blank, two], axis=1)],
+                axis=0,
             )
-            term = weights[slot] * term
+            term = weights[slot] * lax.dot_general(
+                left, right, (((0,), (0,)), ((), ())), preferred_element_type=jnp.float32
+            )
             total = term if total is None else total + term
-        return total
-
-    def compute(chunk, first_y_slot):
+        first, second = total[:, :BLK], total[:, BLK:]
+        square = jnp.where(row_at >= col_at, first, second)
+        diagonal = jnp.sum(jnp.where(row_at == col_at, second, 0.0), axis=0, keepdims=True)
+        return square, diagonal
+
+    def compute_give(chunk):
         for half in range(2):
-            y_order, z_order = spread(y, half), spread(z, half)
-
-            def body(i, carry):
-                z_slot = i % 2
-                y_at = jnp.where(i // 2 == 0, y_order[first_y_slot], y_order[first_y_slot + 1])
-                z_at = jnp.where(z_slot == 0, z_order[2 * chunk], z_order[2 * chunk + 1])
-                column = ((y_at * SIDE + z_at) * OWN + 2 * half) * BLK
-                one, two = gram(column), gram(column + BLK)
-                place = acc.at[half, chunk, first_y_slot + i // 2, z_slot]
-                place[:BLK, :] = jnp.where(row_at >= col_at, one, two)
-                diagonal = jnp.sum(
-                    jnp.where(row_at == col_at, two, 0.0), axis=0, keepdims=True
-                )
-                place[BLK:, :] = jnp.broadcast_to(diagonal, (8, BLK))
-                return carry
-
-            lax.fori_loop(0, 4, body, 0)
+            for i in range(2):
+                square, diagonal = unit(half, y_orders[half][i], z_orders[half][chunk])
+                give[half, chunk, i * BLK:(i + 1) * BLK, :] = square
+                if i == 0:
+                    give[half, chunk, 2 * BLK:, :] = jnp.broadcast_to(diagonal, (8, BLK))
+                else:
+                    give[half, chunk, 2 * BLK + 1:2 * BLK + 2, :] = diagonal
+
+    def compute_keep(chunk):
+        for half in range(2):
+            for i in range(2):
+                square, diagonal = unit(half, y_orders[half][2 + i], z_orders[half][chunk])
+                keep[half, chunk, i, :BLK, :] = square
+                keep[half, chunk, i, BLK:, :] = jnp.broadcast_to(diagonal, (8, BLK))
 
     def remote(src, dst, send, recv, to):
         return pltpu.make_async_remote_copy(
@@ -145,66 +169,78 @@
     z_first = [flip1(z), flip3(z)]
     z_second = [flip3(z), flip1(z)]
     to_s, to_y = final_target(s, y)
-
-    step_y1 = [[remote(acc.at[h, c, pl.ds(0, 2)], got_y1.at[h, c], y1_send.at[h, c],
-                       y1_recv.at[h, c], (s, y_first[h], z)) for c in range(2)] for h in range(2)]
-    step_y2 = [[remote(acc.at[h, c, 2], got_y2.at[h, c], y2_send.at[h, c],
-                       y2_recv.at[h, c], (s, y_second[h], z)) for c in range(2)] for h in range(2)]
-    step_z1 = [remote(acc.at[h, 0, 3], got_z1.at[h], z1_send.at[h], z1_recv.at[h],
-                      (s, y, z_first[h])) for h in range(2)]
-    step_f = [[remote(acc.at[h, 1, 3, 0], got_f.at[h, 0], f_send.at[h, 0], f_recv.at[h, 0],
-                      (to_s, to_y, z_second[h])),
-               remote(acc.at[h, 1, 3, 1], got_f.at[h, 1], f_send.at[h, 1], f_recv.at[h, 1],
-                      (to_s, to_y, z))] for h in range(2)]
-
-    for part in range(2):
-        fetch(sent_act.at[0], part).wait()
-    compute(0, 0)
+    halves, chunks = range(2), range(SIDE)
+
+    step_y1 = [[remote(give.at[h, c], got_y1.at[h, c], y1_send.at[h, c], y1_recv.at[h, c],
+                       (s, y_first[h], z)) for c in chunks] for h in halves]
+    step_y2 = [[remote(keep.at[h, c, 0], got_y2.at[h, c], y2_send.at[h, c], y2_recv.at[h, c],
+                       (s, y_second[h], z)) for c in chunks] for h in halves]
+    step_z1 = [remote(keep.at[h, 0, 1], got_z1.at[h], z1_send.at[h], z1_recv.at[h],
+                      (s, y, z_first[h])) for h in halves]
+    step_f = [[remote(keep.at[h, 1 + j, 1], got_f.at[h, j], f_send.at[h, j], f_recv.at[h, j],
+                      (to_s, to_y, to_z))
+               for j, to_z in enumerate((z_first[h], z_second[h], z))] for h in halves]
+
+    def add_first(h, c, i):
+        keep[h, c, i, :BLK] = keep[h, c, i, :BLK] + got_y1[h, c, i * BLK:(i + 1) * BLK]
+        at = 2 * BLK + i
+        keep[h, c, i, BLK:BLK + 1] = keep[h, c, i, BLK:BLK + 1] + got_y1[h, c, at:at + 1]
+
+    def finish(c):
+        for h in halves:
+            step_y2[h][c].wait_recv()
+            if c == 2:
+                step_z1[h].wait_recv()
+                keep[h, c, 1] = keep[h, c, 1] + (got_y2[h, c] + got_z1[h])
+            else:
+                keep[h, c, 1] = keep[h, c, 1] + got_y2[h, c]
+            (step_z1[h] if c == 0 else step_f[h][c - 1]).start()
+
+    fetched(0)
+    compute_give(0)
     pl.semaphore_wait(barrier, len(greet))
-    for h in range(2):
+    for h in halves:
         step_y1[h][0].start()
-    compute(1, 0)
-    for h in range(2):
+    fetched(1)
+    fetched(2)
+    compute_give(1)
+    for h in halves:
         step_y1[h][1].start()
-    compute(0, 2)
-    compute(1, 2)
-
-    for c in range(2):
-        for h in range(2):
+    compute_give(2)
+    fetched(3)
+    for c in chunks:
+        if c == 1:
+            compute_give(3)
+        compute_keep(c)
+        for h in halves:
             step_y1[h][c].wait_recv()
-            acc[h, c, 2] = acc[h, c, 2] + got_y1[h, c, 0]
+            add_first(h, c, 0)
             step_y2[h][c].start()
-            acc[h, c, 3] = acc[h, c, 3] + got_y1[h, c, 1]
-    for h in range(2):
-        step_y2[h][0].wait_recv()
-        acc[h, 0, 3] = acc[h, 0, 3] + got_y2[h, 0]
-        step_z1[h].start()
-    for h in range(2):
-        step_y2[h][1].wait_recv()
-        acc[h, 1, 3] = acc[h, 1, 3] + got_y2[h, 1]
-    for h in range(2):
-        step_z1[h].wait_recv()
-        for i in range(2):
-            acc[h, 1, 3, i] = acc[h, 1, 3, i] + got_z1[h, i]
-            step_f[h][i].start()
-    for h in range(2):
-        for c in range(2):
+            if c + 2 < SIDE:
+                step_y1[h][c + 2].start()
+            add_first(h, c, 1)
+        if c > 0:
+            finish(c - 1)
+    finish(SIDE - 1)
+    for h in halves:
+        for c in chunks:
             step_y1[h][c].wait_send()
             step_y2[h][c].wait_send()
         step_z1[h].wait_send()
-    for h in range(2):
-        for i in range(2):
-            step_f[h][i].wait_recv()
-        out[h] = got_f[h, 0] + got_f[h, 1]
-    for h in range(2):
-        for i in range(2):
-            step_f[h][i].wait_send()
+    for h in halves:
+        for j in range(3):
+            step_f[h][j].wait_recv()
+        out[h] = got_f[h, 0] + got_f[h, 1] + got_f[h, 2]
+    for h in halves:
+        for j in range(3):
+            step_f[h][j].wait_send()
 
 
 def reduce_blocks(sent_act, sent_grad, embedded, loss_grad, micro_weight, order):
     dma = pltpu.SemaphoreType.DMA
     block = (PACKED, BLK)
-    hbm, smem = pl.BlockSpec(memory_space=pl.ANY), pl.BlockSpec(memory_space=pltpu.SMEM)
+    pair = (2 * BLK + 8, BLK)
+    hbm, smem = pl.BlockSpec(memory_space=pltpu.HBM), pl.BlockSpec(memory_space=pltpu.SMEM)
     return pl.pallas_call(
         reduce_kernel,
         out_shape=jax.ShapeDtypeStruct((2,) + block, jnp.float32),
@@ -212,17 +248,18 @@
         out_specs=pl.BlockSpec(memory_space=pltpu.VMEM),
         scratch_shapes=[
             pltpu.VMEM((ROWS, 2 * D), jnp.bfloat16),
-            pltpu.VMEM((2, 2, 4, 2) + block, jnp.float32),
-            pltpu.VMEM((2, 2, 2, 2) + block, jnp.float32),
-            pltpu.VMEM((2, 2, 2) + block, jnp.float32),
-            pltpu.VMEM((2, 2) + block, jnp.float32),
-            pltpu.VMEM((2, 2) + block, jnp.float32),
-            dma((2,)),
-            dma((2, 2)), dma((2, 2)), dma((2, 2)), dma((2, 2)),
-            dma((2,)), dma((2,)), dma((2, 2)), dma((2, 2)),
+            pltpu.VMEM((2, SIDE) + pair, jnp.float32),
+            pltpu.VMEM((2, SIDE, 2) + block, jnp.float32),
+            pltpu.VMEM((2, SIDE) + pair, jnp.float32),
+            pltpu.VMEM((2, SIDE) + block, jnp.float32),
+            pltpu.VMEM((2,) + block, jnp.float32),
+            pltpu.VMEM((2, 3) + block, jnp.float32),
+            dma((SIDE, SIDE)),
+            dma((2, SIDE)), dma((2, SIDE)), dma((2, SIDE)), dma((2, SIDE)),
+            dma((2,)), dma((2,)), dma((2, 3)), dma((2, 3)),
         ],
         compiler_params=pltpu.CompilerParams(
-            collective_id=0, has_side_effects=True, vmem_limit_bytes=32 * 1024 * 1024
+            collective_id=0, has_side_effects=True, vmem_limit_bytes=VMEM_LIMIT
         ),
         name="gram_reduce",
     )(sent_act, sent_grad, embedded, loss_grad, micro_weight, order)
@@ -305,13 +342,14 @@
         in_specs=[vmem, smem, vmem, vmem],
         out_specs=vmem,
         scratch_shapes=[pltpu.VMEM((OWN, BLK, BLK), jnp.float32)],
-        compiler_params=pltpu.CompilerParams(vmem_limit_bytes=32 * 1024 * 1024),
+        compiler_params=pltpu.CompilerParams(vmem_limit_bytes=VMEM_LIMIT),
         name="invert",
     )(micro_weight, assignment, packed, old_inverse)
 
 
 def shards(sent_act, sent_grad, embedded, loss_grad, micro_weight, order, assignment, old_inverse):
-    packed = reduce_blocks(sent_act, sent_grad, embedded, loss_grad, micro_weight, order)
+    micro_weight = micro_weight.T
+    packed = reduce_blocks(sent_act, sent_grad, embedded, loss_grad, micro_weight, order.T)
     return invert_blocks(micro_weight, assignment, packed, old_inverse)
 
 

time: 57.6 us -> 43.7 us (0.76)
  local copies, waits for them, and re-layouts: 7.88 us -> 0 us
  Pallas kernels: 49.4 us -> 43.6 us
    unnamed x14 -> x0, local copies, waits for them, and re-layouts: 7.88 us -> none
    pallas_call x1, Pallas kernels: 41.9 us -> 35.5 us  [reduce_blocks(): pl.pallas_call(reduce_kernel, out_shape=jax.ShapeDtypeStruct((2,) + block...]
where the time goes in v2:
time: 43.7 us; the launch traced here: 43.6 us
  Pallas kernels  43.6 us (100%)
    pallas_call x1, Pallas kernels, reduce_blocks(): pl.pallas_call(reduce_kernel, out_shape=jax.ShapeDtypeStruct((2,) + block...  35.5 us
    pallas_call x1, Pallas kernels, invert_blocks(): pl.pallas_call(invert_kernel, out_shape=jax.ShapeDtypeStruct(old_inverse....  8.05 us

profile of v2, /device:TPU:1, one launch (start us, length us, event | category | flops | bytes accessed | tf_op | source)
XLA Modules:
  0.0 43.6 jit_solution(2470780561510324613)
XLA Ops:
  0.0 35.5 %gram_reduce.1.packed = f32[2,136,128]{2,1,0:T(8,128)} custom-call(bf16[1,256,4096]{2,1,0:T(8,128)(2,1)} %sent_act.1, bf16[1,256,4096]{2,1,0:T(8,128)(2,1)} %sent_grad.1, bf16[256,4096]{1,0:T(8,128)(2,1)} %embedded.1, bf16[256,4096]{1,0:T(8,128)(2,1)} %loss_grad.1, f32[4,16]{1,0:T(4,128)} %bitcast.2, s32[4,16]{1,0:T(4,128)} %bitcast.4), custom_call_target="tpu_custom_call" | custom-call | tf_op jit(solution)/shard_map/gram_reduce/pallas_call | solution.py:244
  35.5 8.1 %invert.1 = f32[1,4,128,128]{3,2,1,0:T(8,128)} custom-call(f32[4,16]{1,0:T(4,128)} %bitcast.3, s32[1,64]{1,0:T(1,128)} %assignment.1, f32[2,136,128]{2,1,0:T(8,128)} %gram_reduce.1.packed, f32[1,4,128,128]{3,2,1,0:T(8,128)} %old.1), custom_call_target="tpu_custom_call" | custom-call | tf_op jit(solution)/shard_map/invert/pallas_call | solution.py:339

commit v3 on v2

--- a/solution.py
+++ b/solution.py
@@ -16,7 +16,11 @@
 SECTIONS = 16
 REPLICAS = 16
 PACKED = BLK + 8
+TOP = 88
+LOW = BLK - TOP
 PANEL = 8
+ROUNDS = 2
+LIMIT = 1e-6
 VMEM_LIMIT = 60 * 1024 * 1024
 MESH = pl.DeviceIdType.MESH
 
@@ -57,46 +61,14 @@
 
 def reduce_kernel(
     sent_act, sent_grad, embedded, loss_grad, micro_weight, order, out,
-    rows, give, keep, got_y1, got_y2, got_z1, got_f, in_sem,
+    rows, give, keep, got_y1, got_y2, got_z1, got_f,
+    low_give, low_keep, low_z1, low_y1, low_y2, low_f, in_sem,
     y1_send, y1_recv, y2_send, y2_recv, z1_send, z1_recv, f_send, f_recv,
+    lz1_send, lz1_recv, ly1_send, ly1_recv, ly2_send, ly2_recv, lf_send, lf_recv,
 ):
     s = lax.axis_index("section")
     r = lax.axis_index("dp")
     y, z = r // SIDE, r % SIDE
-    fetch_order = (flip2(z), flip1(z), flip3(z), z)
-
-    def fetch(src, to_y, place):
-        column = (to_y * SIDE + fetch_order[place]) * OWN * BLK
-        wide = pl.ds(pl.multiple_of(column, OWN * BLK), OWN * BLK)
-        narrow = pl.ds(pl.multiple_of(column - to_y // 2 * D, OWN * BLK), OWN * BLK)
-        return pltpu.make_async_copy(
-            src.at[:, narrow], rows.at[:, wide], in_sem.at[place, to_y]
-        )
-
-    for place in range(SIDE):
-        @pl.when(s < SECTIONS - 1)
-        def _():
-            for to_y in range(2):
-                fetch(sent_act.at[0], to_y, place).start()
-
-        @pl.when(s == SECTIONS - 1)
-        def _():
-            for to_y in range(2):
-                fetch(loss_grad, to_y, place).start()
-
-        @pl.when(s > 0)
-        def _():
-            for to_y in range(2, 4):
-                fetch(sent_grad.at[0], to_y, place).start()
-
-        @pl.when(s == 0)
-        def _():
-            for to_y in range(2, 4):
-                fetch(embedded, to_y, place).start()
-
-    def fetched(place):
-        for to_y in range(SIDE):
-            fetch(sent_act.at[0], to_y, place).wait()
 
     barrier = pltpu.get_barrier_semaphore()
     from_s, from_y = final_source(s, y)
@@ -106,6 +78,41 @@
         pl.semaphore_signal(
             barrier, inc=1, device_id=(to_s, to_y * SIDE + to_z), device_id_type=MESH
         )
+
+    fetch_order = (flip2(z), flip1(z), flip3(z), z)
+
+    def fetch(src, to_y, place):
+        column = (to_y * SIDE + fetch_order[place]) * OWN * BLK
+        wide = pl.ds(pl.multiple_of(column, OWN * BLK), OWN * BLK)
+        narrow = pl.ds(pl.multiple_of(column - to_y // 2 * D, OWN * BLK), OWN * BLK)
+        return pltpu.make_async_copy(
+            src.at[:, narrow], rows.at[:, wide], in_sem.at[place, to_y]
+        )
+
+    for place in range(SIDE):
+        @pl.when(s < SECTIONS - 1)
+        def _():
+            for to_y in range(2):
+                fetch(sent_act.at[0], to_y, place).start()
+
+        @pl.when(s == SECTIONS - 1)
+        def _():
+            for to_y in range(2):
+                fetch(loss_grad, to_y, place).start()
+
+        @pl.when(s > 0)
+        def _():
+            for to_y in range(2, 4):
+                fetch(sent_grad.at[0], to_y, place).start()
+
+        @pl.when(s == 0)
+        def _():
+            for to_y in range(2, 4):
+                fetch(embedded, to_y, place).start()
+
+    def fetched(place):
+        for to_y in range(SIDE):
+            fetch(sent_act.at[0], to_y, place).wait()
 
     weights = []
     for slot in range(MB):
@@ -141,22 +148,21 @@
         diagonal = jnp.sum(jnp.where(row_at == col_at, second, 0.0), axis=0, keepdims=True)
         return square, diagonal
 
-    def compute_give(chunk):
+    def compute(chunk):
         for half in range(2):
-            for i in range(2):
+            for i in range(SIDE):
                 square, diagonal = unit(half, y_orders[half][i], z_orders[half][chunk])
-                give[half, chunk, i * BLK:(i + 1) * BLK, :] = square
-                if i == 0:
-                    give[half, chunk, 2 * BLK:, :] = jnp.broadcast_to(diagonal, (8, BLK))
+                top, bottom = square[:TOP], square[TOP:]
+                if i < 2:
+                    give[half, chunk, i * TOP:(i + 1) * TOP, :] = top
+                    if i == 0:
+                        give[half, chunk, 2 * TOP:, :] = jnp.broadcast_to(diagonal, (8, BLK))
+                    else:
+                        give[half, chunk, 2 * TOP + 1:2 * TOP + 2, :] = diagonal
                 else:
-                    give[half, chunk, 2 * BLK + 1:2 * BLK + 2, :] = diagonal
-
-    def compute_keep(chunk):
-        for half in range(2):
-            for i in range(2):
-                square, diagonal = unit(half, y_orders[half][2 + i], z_orders[half][chunk])
-                keep[half, chunk, i, :BLK, :] = square
-                keep[half, chunk, i, BLK:, :] = jnp.broadcast_to(diagonal, (8, BLK))
+                    keep[half, chunk, i - 2, :TOP, :] = top
+                    keep[half, chunk, i - 2, TOP:, :] = jnp.broadcast_to(diagonal, (8, BLK))
+                (low_give if chunk < 2 else low_keep)[half, i, chunk % 2] = bottom
 
     def remote(src, dst, send, recv, to):
         return pltpu.make_async_remote_copy(
@@ -180,13 +186,31 @@
     step_f = [[remote(keep.at[h, 1 + j, 1], got_f.at[h, j], f_send.at[h, j], f_recv.at[h, j],
                       (to_s, to_y, to_z))
                for j, to_z in enumerate((z_first[h], z_second[h], z))] for h in halves]
+    low_step_z1 = [[remote(low_give.at[h, i], low_z1.at[h, i], lz1_send.at[h, i],
+                           lz1_recv.at[h, i], (s, y, z_first[h])) for i in chunks] for h in halves]
+    low_step_y1 = [[remote(low_keep.at[h, i], low_y1.at[h, i], ly1_send.at[h, i],
+                           ly1_recv.at[h, i], (s, y_first[h], z)) for i in range(2)] for h in halves]
+    low_step_y2 = [remote(low_keep.at[h, 2], low_y2.at[h], ly2_send.at[h], ly2_recv.at[h],
+                          (s, y_second[h], z)) for h in halves]
+    low_step_f = [[remote(low_keep.at[h, 3, j], low_f.at[h, j], lf_send.at[h, j],
+                          lf_recv.at[h, j], (to_s, to_y, to_z))
+                   for j, to_z in enumerate((z_second[h], z))] for h in halves]
 
     def add_first(h, c, i):
-        keep[h, c, i, :BLK] = keep[h, c, i, :BLK] + got_y1[h, c, i * BLK:(i + 1) * BLK]
-        at = 2 * BLK + i
-        keep[h, c, i, BLK:BLK + 1] = keep[h, c, i, BLK:BLK + 1] + got_y1[h, c, at:at + 1]
-
-    def finish(c):
+        keep[h, c, i, :TOP] = keep[h, c, i, :TOP] + got_y1[h, c, i * TOP:(i + 1) * TOP]
+        at = 2 * TOP + i
+        keep[h, c, i, TOP:TOP + 1] = keep[h, c, i, TOP:TOP + 1] + got_y1[h, c, at:at + 1]
+
+    def after_y1(c):
+        for h in halves:
+            step_y1[h][c].wait_recv()
+            add_first(h, c, 0)
+            step_y2[h][c].start()
+            if c + 2 < SIDE:
+                step_y1[h][c + 2].start()
+            add_first(h, c, 1)
+
+    def after_y2(c):
         for h in halves:
             step_y2[h][c].wait_recv()
             if c == 2:
@@ -196,54 +220,92 @@
                 keep[h, c, 1] = keep[h, c, 1] + got_y2[h, c]
             (step_z1[h] if c == 0 else step_f[h][c - 1]).start()
 
+    def after_low_z1(i):
+        for h in halves:
+            low_step_z1[h][i].wait_recv()
+            low_keep[h, i] = low_keep[h, i] + low_z1[h, i]
+            if i < 2:
+                low_step_y1[h][i].start()
+
+    def after_low_y1():
+        for h in halves:
+            for i in range(2):
+                low_step_y1[h][i].wait_recv()
+                low_keep[h, 2 + i] = low_keep[h, 2 + i] + low_y1[h, i]
+                if i == 0:
+                    low_step_y2[h].start()
+
+    def after_low_y2():
+        for h in halves:
+            low_step_y2[h].wait_recv()
+            low_keep[h, 3] = low_keep[h, 3] + low_y2[h]
+            for j in range(2):
+                low_step_f[h][j].start()
+
     fetched(0)
-    compute_give(0)
+    compute(0)
     pl.semaphore_wait(barrier, len(greet))
     for h in halves:
         step_y1[h][0].start()
     fetched(1)
     fetched(2)
-    compute_give(1)
+    compute(1)
     for h in halves:
         step_y1[h][1].start()
-    compute_give(2)
+        for i in chunks:
+            low_step_z1[h][i].start()
+    compute(2)
     fetched(3)
-    for c in chunks:
-        if c == 1:
-            compute_give(3)
-        compute_keep(c)
-        for h in halves:
-            step_y1[h][c].wait_recv()
-            add_first(h, c, 0)
-            step_y2[h][c].start()
-            if c + 2 < SIDE:
-                step_y1[h][c + 2].start()
-            add_first(h, c, 1)
-        if c > 0:
-            finish(c - 1)
-    finish(SIDE - 1)
+    compute(3)
+    after_y1(0)
+    after_low_z1(0)
+    after_low_z1(1)
+    after_y1(1)
+    after_y2(0)
+    after_low_z1(2)
+    after_low_z1(3)
+    after_y1(2)
+    after_low_y1()
+    after_y2(1)
+    after_y1(3)
+    after_low_y2()
+    after_y2(2)
+    after_y2(3)
     for h in halves:
         for c in chunks:
             step_y1[h][c].wait_send()
             step_y2[h][c].wait_send()
+            low_step_z1[h][c].wait_send()
         step_z1[h].wait_send()
+        low_step_y1[h][0].wait_send()
+        low_step_y1[h][1].wait_send()
+        low_step_y2[h].wait_send()
+    for h in halves:
+        for j in range(2):
+            low_step_f[h][j].wait_recv()
+        out[h, TOP:BLK] = low_f[h, 0] + low_f[h, 1]
     for h in halves:
         for j in range(3):
             step_f[h][j].wait_recv()
-        out[h] = got_f[h, 0] + got_f[h, 1] + got_f[h, 2]
+        total = got_f[h, 0] + got_f[h, 1] + got_f[h, 2]
+        out[h, :TOP] = total[:TOP]
+        out[h, BLK:] = total[TOP:]
     for h in halves:
         for j in range(3):
             step_f[h][j].wait_send()
+        for j in range(2):
+            low_step_f[h][j].wait_send()
 
 
 def reduce_blocks(sent_act, sent_grad, embedded, loss_grad, micro_weight, order):
     dma = pltpu.SemaphoreType.DMA
-    block = (PACKED, BLK)
-    pair = (2 * BLK + 8, BLK)
+    block = (TOP + 8, BLK)
+    pair = (2 * TOP + 8, BLK)
+    low = (2, LOW, BLK)
     hbm, smem = pl.BlockSpec(memory_space=pltpu.HBM), pl.BlockSpec(memory_space=pltpu.SMEM)
     return pl.pallas_call(
         reduce_kernel,
-        out_shape=jax.ShapeDtypeStruct((2,) + block, jnp.float32),
+        out_shape=jax.ShapeDtypeStruct((2, PACKED, BLK), jnp.float32),
         in_specs=[hbm] * 4 + [smem] * 2,
         out_specs=pl.BlockSpec(memory_space=pltpu.VMEM),
         scratch_shapes=[
@@ -254,9 +316,17 @@
             pltpu.VMEM((2, SIDE) + block, jnp.float32),
             pltpu.VMEM((2,) + block, jnp.float32),
             pltpu.VMEM((2, 3) + block, jnp.float32),
+            pltpu.VMEM((2, SIDE) + low, jnp.float32),
+            pltpu.VMEM((2, SIDE) + low, jnp.float32),
+            pltpu.VMEM((2, SIDE) + low, jnp.float32),
+            pltpu.VMEM((2, 2) + low, jnp.float32),
+            pltpu.VMEM((2,) + low, jnp.float32),
+            pltpu.VMEM((2,) + low, jnp.float32),
             dma((SIDE, SIDE)),
             dma((2, SIDE)), dma((2, SIDE)), dma((2, SIDE)), dma((2, SIDE)),
             dma((2,)), dma((2,)), dma((2, 3)), dma((2, 3)),
+            dma((2, SIDE)), dma((2, SIDE)), dma((2, 2)), dma((2, 2)),
+            dma((2,)), dma((2,)), dma((2, 2)), dma((2, 2)),
         ],
         compiler_params=pltpu.CompilerParams(
             collective_id=0, has_side_effects=True, vmem_limit_bytes=VMEM_LIMIT
@@ -273,26 +343,30 @@
     return high, middle, low
 
 
-def invert_kernel(micro_weight, assignment, packed, old, out, work):
-    r = lax.axis_index("dp")
-    row_at = lax.broadcasted_iota(jnp.int32, (BLK, BLK), 0)
-    col_at = lax.broadcasted_iota(jnp.int32, (BLK, BLK), 1)
-    weight_sum = jnp.sum(
-        jnp.sum(micro_weight[...], axis=1, keepdims=True), axis=0, keepdims=True
-    )
-    scale = 1.0 / (MROWS * weight_sum)
-    shift = jnp.where(row_at == col_at, jnp.float32(damping), 0.0)
-    for half in range(2):
-        square = packed[half, :BLK, :]
-        flipped = square.T
-        one = jnp.where(row_at >= col_at, square, flipped)
-        two = jnp.where(row_at < col_at, square, flipped)
-        two = jnp.where(row_at == col_at, packed[half, BLK:BLK + 1, :], two)
-        work[2 * half] = one * scale + shift
-        work[2 * half + 1] = two * scale + shift
-
+def dot(x, y):
+    return lax.dot_general(x, y, (((1,), (0,)), ((), ())), preferred_element_type=jnp.float32)
+
+
+def narrow(x):
+    return x.astype(jnp.bfloat16)
+
+
+def total(x):
+    return jnp.sum(jnp.sum(x, axis=0, keepdims=True), axis=1, keepdims=True)
+
+
+def dot_exact(x, y):
+    h0, m0, l0 = split3(x)
+    h1, m1, l1 = split3(y)
+    left = jnp.concatenate([l0, h0, m0, m0, h0, h0], axis=1)
+    right = jnp.concatenate([h1, l1, m1, h1, m1, h1], axis=0)
+    return dot(left, right)
+
+
+def sweep(work):
     sub = lax.broadcasted_iota(jnp.int32, (PANEL, BLK), 0)
     lane = lax.broadcasted_iota(jnp.int32, (PANEL, BLK), 1)
+    col_at = lax.broadcasted_iota(jnp.int32, (BLK, BLK), 1)
 
     def spread_row(x, k):
         return jnp.broadcast_to(x[k:k + 1, :], (PANEL, BLK))
@@ -329,19 +403,88 @@
             work[m] = jnp.where(panel_cols, 0.0, work[m]) - update
             work[m, start:start + PANEL, :] = swept
 
-    for m in range(OWN):
-        refreshed = assignment[0, r * OWN + m] < REPLICAS
-        out[0, m] = jnp.where(refreshed, -work[m], old[0, m])
+
+def invert_kernel(micro_weight, assignment, packed, old_hbm, out_hbm, work, old, out, mask, sems):
+    r = lax.axis_index("dp")
+    get_old = pltpu.make_async_copy(old_hbm, old, sems.at[0])
+    get_mask = pltpu.make_async_copy(assignment, mask, sems.at[1])
+    get_old.start()
+    get_mask.start()
+    row_at = lax.broadcasted_iota(jnp.int32, (BLK, BLK), 0)
+    col_at = lax.broadcasted_iota(jnp.int32, (BLK, BLK), 1)
+    on_diagonal = row_at == col_at
+    identity = jnp.where(on_diagonal, 1.0, 0.0)
+    scale = 1.0 / (MROWS * total(micro_weight[...]))
+    for half in range(2):
+        square = packed[half, :BLK, :]
+        flipped = square.T
+        one = jnp.where(row_at >= col_at, square, flipped)
+        two = jnp.where(row_at < col_at, square, flipped)
+        two = jnp.where(on_diagonal, packed[half, BLK:BLK + 1, :], two)
+        work[2 * half] = one * scale + damping * identity
+        work[2 * half + 1] = two * scale + damping * identity
+
+    every = range(OWN)
+    factors = [work[m] for m in every]
+    spots = [jnp.where(on_diagonal, x, 0.0) for x in factors]
+    along = [lax.rsqrt(jnp.sum(x, axis=0, keepdims=True)) for x in spots]
+    down = [lax.rsqrt(jnp.sum(x, axis=1, keepdims=True)) for x in spots]
+    unit = [factors[m] * along[m] * down[m] for m in every]
+    gains = [BLK / total(x * x) for x in unit]
+    power = [identity - gains[m] * unit[m] for m in every]
+    series = [identity + x for x in power]
+    power = [dot(narrow(x), narrow(x)) for x in power]
+    for _ in range(ROUNDS):
+        both = [
+            dot(narrow(power[m]),
+                jnp.concatenate([narrow(power[m]), narrow(series[m])], axis=1)) for m in every
+        ]
+        series = [series[m] + both[m][:, BLK:] for m in every]
+        power = [x[:, :BLK] for x in both]
+    series = [series[m] + dot(narrow(power[m]), narrow(series[m])) for m in every]
+    guess = [gains[m] * series[m] for m in every]
+    rest = [identity - dot_exact(unit[m], guess[m]) for m in every]
+    square = [dot(narrow(x), narrow(x)) for x in rest]
+    size = [total(x * x) for x in square]
+    worst = jnp.maximum(jnp.maximum(size[0], size[1]), jnp.maximum(size[2], size[3]))
+    square = [square[m] + dot(narrow(square[m]), narrow(rest[m])) for m in every]
+    change = [rest[m] + square[m] for m in every]
+    fresh = [guess[m] + dot_exact(guess[m], change[m]) for m in every]
+    for m in every:
+        out[0, m] = fresh[m] * along[m] * down[m]
+
+    @pl.when(jnp.logical_not(worst[0, 0] <= LIMIT))
+    def _():
+        sweep(work)
+        for m in every:
+            out[0, m] = -work[m]
+
+    get_old.wait()
+    get_mask.wait()
+    puts = []
+    for m in every:
+        refreshed = mask[0, r * OWN + m] < REPLICAS
+        out[0, m] = jnp.where(refreshed, out[0, m], old[0, m])
+        puts.append(pltpu.make_async_copy(out.at[0, m], out_hbm.at[0, m], sems.at[2 + m]))
+        puts[m].start()
+    for put in puts:
+        put.wait()
 
 
 def invert_blocks(micro_weight, assignment, packed, old_inverse):
-    vmem, smem = pl.BlockSpec(memory_space=pltpu.VMEM), pl.BlockSpec(memory_space=pltpu.SMEM)
+    vmem, hbm = pl.BlockSpec(memory_space=pltpu.VMEM), pl.BlockSpec(memory_space=pltpu.HBM)
     return pl.pallas_call(
         invert_kernel,
         out_shape=jax.ShapeDtypeStruct(old_inverse.shape, jnp.float32),
-        in_specs=[vmem, smem, vmem, vmem],
-        out_specs=vmem,
-        scratch_shapes=[pltpu.VMEM((OWN, BLK, BLK), jnp.float32)],
+        in_specs=[vmem, hbm, vmem, hbm],
+        out_specs=hbm,
+        scratch_shapes=[
+            pltpu.VMEM((OWN, BLK, BLK), jnp.float32),
+            pltpu.VMEM((1, OWN, BLK, BLK), jnp.float32),
+            pltpu.VMEM((1, OWN, BLK, BLK), jnp.float32),
+            pltpu.SMEM((1, NBLK), jnp.int32),
+            pltpu.SemaphoreType.DMA((2 + OWN,)),
+        ],
         compiler_params=pltpu.CompilerParams(vmem_limit_bytes=VMEM_LIMIT),
         name="invert",
     )(micro_weight, assignment, packed, old_inverse)

time: 43.7 us -> 44.3 us (1.014)
  Pallas kernels: 43.6 us -> 44.1 us
    pallas_call x1, Pallas kernels: 8.05 us -> 9.81 us  [invert_blocks(): pl.pallas_call(invert_kernel, out_shape=jax.ShapeDtypeStruct(old_inverse....]
    pallas_call x1, Pallas kernels: 35.5 us -> 34.3 us  [reduce_blocks(): pl.pallas_call(reduce_kernel, out_shape=jax.ShapeDtypeStruct((2, PACKED,...]
where the time goes in v3:
time: 44.3 us; the launch traced here: 44.1 us
  Pallas kernels  44.1 us (100%)
    pallas_call x1, Pallas kernels, reduce_blocks(): pl.pallas_call(reduce_kernel, out_shape=jax.ShapeDtypeStruct((2, PACKED,...  34.3 us
    pallas_call x1, Pallas kernels, invert_blocks(): pl.pallas_call(invert_kernel, out_shape=jax.ShapeDtypeStruct(old_inverse....  9.81 us

profile of v3, /device:TPU:1, one launch (start us, length us, event | category | flops | bytes accessed | tf_op | source)
XLA Modules:
  0.0 44.1 jit_solution(8001690746901128323)
XLA Ops:
  0.0 34.3 %gram_reduce.1.packed = f32[2,136,128]{2,1,0:T(8,128)} custom-call(bf16[1,256,4096]{2,1,0:T(8,128)(2,1)} %sent_act.1, bf16[1,256,4096]{2,1,0:T(8,128)(2,1)} %sent_grad.1, bf16[256,4096]{1,0:T(8,128)(2,1)} %embedded.1, bf16[256,4096]{1,0:T(8,128)(2,1)} %loss_grad.1, f32[4,16]{1,0:T(4,128)} %bitcast.2, s32[4,16]{1,0:T(4,128)} %bitcast.4), custom_call_target="tpu_custom_call" | custom-call | tf_op jit(solution)/shard_map/gram_reduce/pallas_call | solution.py:306
  34.3 9.8 %invert.1 = f32[1,4,128,128]{3,2,1,0:T(8,128)} custom-call(f32[4,16]{1,0:T(4,128)} %bitcast.3, s32[1,64]{1,0:T(1,128)} %assignment.1, f32[2,136,128]{2,1,0:T(8,128)} %gram_reduce.1.packed, f32[1,4,128,128]{3,2,1,0:T(8,128)} %old_hbm.1), custom_call_target="tpu_custom_call" | custom-call | tf_op jit(solution)/shard_map/invert/pallas_call | solution.py:476

commit v4 on v3

--- a/solution.py
+++ b/solution.py
@@ -16,8 +16,18 @@
 SECTIONS = 16
 REPLICAS = 16
 PACKED = BLK + 8
-TOP = 88
-LOW = BLK - TOP
+QUARTER = BLK // 4
+CODED = 3 * QUARTER
+BITS = 22.0
+GROUPS = ((0,), (1,), (2,), (3,))
+
+
+def message_rows(units):
+    return units * CODED + -(-3 * units // 8) * 8
+
+
+GIVE_AT = [sum(message_rows(2 * len(g)) for g in GROUPS[:i]) for i in range(len(GROUPS) + 1)]
+PASS_AT = [sum(message_rows(len(g)) for g in GROUPS[:i]) for i in range(len(GROUPS) + 1)]
 PANEL = 8
 ROUNDS = 2
 LIMIT = 1e-6
@@ -59,12 +69,36 @@
     return from_s, from_y
 
 
+def encode(square, diagonal, row_at, col_at):
+    first = jnp.sum(jnp.where(row_at == col_at, square, 0.0), axis=0, keepdims=True)
+    marks = []
+    for entry in (first, diagonal):
+        entry = jnp.maximum(entry, 1e-30)
+        largest = jnp.max(entry, axis=1, keepdims=True)
+        marks.append(jnp.ceil(0.5 * (jnp.log2(entry) + jnp.log2(largest))))
+    gain = [jnp.exp2(BITS - mark) for mark in marks]
+    values = (square * jnp.where(row_at >= col_at, gain[0], gain[1])).astype(jnp.int32)
+    part = [values[i * QUARTER:(i + 1) * QUARTER] for i in range(4)]
+    words = [(part[i] << 8) | ((part[3] >> (8 * i)) & 255) for i in range(3)]
+    fine = (diagonal * (gain[1] * 256.0)).astype(jnp.int32)
+    return (jnp.concatenate(words, axis=0),
+            (marks[0].astype(jnp.int32), marks[1].astype(jnp.int32), fine))
+
+
+def decode(words, marks, row_at, col_at):
+    part = [words[i * QUARTER:(i + 1) * QUARTER] for i in range(3)]
+    last = (part[0] & 255) | ((part[1] & 255) << 8) | ((part[2] & 255) << 16)
+    values = jnp.concatenate([x >> 8 for x in part] + [(last << 8) >> 8], axis=0)
+    step = [jnp.exp2(mark.astype(jnp.float32) - BITS) for mark in marks[:2]]
+    square = values.astype(jnp.float32) * jnp.where(row_at >= col_at, step[0], step[1])
+    return square, marks[2].astype(jnp.float32) * (step[1] * (1.0 / 256.0))
+
+
 def reduce_kernel(
     sent_act, sent_grad, embedded, loss_grad, micro_weight, order, out,
-    rows, give, keep, got_y1, got_y2, got_z1, got_f,
-    low_give, low_keep, low_z1, low_y1, low_y2, low_f, in_sem,
+    rows, give, pass_on, coded, keep, got_y1, got_y2, got_z1, got_f,
+    weight_table, order_table, in_sem, table_sem,
     y1_send, y1_recv, y2_send, y2_recv, z1_send, z1_recv, f_send, f_recv,
-    lz1_send, lz1_recv, ly1_send, ly1_recv, ly2_send, ly2_recv, lf_send, lf_recv,
 ):
     s = lax.axis_index("section")
     r = lax.axis_index("dp")
@@ -79,17 +113,21 @@
             barrier, inc=1, device_id=(to_s, to_y * SIDE + to_z), device_id_type=MESH
         )
 
-    fetch_order = (flip2(z), flip1(z), flip3(z), z)
+    tables = [
+        pltpu.make_async_copy(micro_weight, weight_table, table_sem.at[0]),
+        pltpu.make_async_copy(order, order_table, table_sem.at[1]),
+    ]
 
     def fetch(src, to_y, place):
-        column = (to_y * SIDE + fetch_order[place]) * OWN * BLK
-        wide = pl.ds(pl.multiple_of(column, OWN * BLK), OWN * BLK)
-        narrow = pl.ds(pl.multiple_of(column - to_y // 2 * D, OWN * BLK), OWN * BLK)
+        pair = (z // 2 + 1 + place) % 2
+        column = (to_y * SIDE + pair * 2) * OWN * BLK
+        wide = pl.ds(pl.multiple_of(column, 2 * OWN * BLK), 2 * OWN * BLK)
+        narrow = pl.ds(pl.multiple_of(column - to_y // 2 * D, 2 * OWN * BLK), 2 * OWN * BLK)
         return pltpu.make_async_copy(
             src.at[:, narrow], rows.at[:, wide], in_sem.at[place, to_y]
         )
 
-    for place in range(SIDE):
+    for place in range(2):
         @pl.when(s < SECTIONS - 1)
         def _():
             for to_y in range(2):
@@ -110,16 +148,22 @@
             for to_y in range(2, 4):
                 fetch(embedded, to_y, place).start()
 
+        if place == 0:
+            for table in tables:
+                table.start()
+
     def fetched(place):
         for to_y in range(SIDE):
             fetch(sent_act.at[0], to_y, place).wait()
 
+    for table in tables:
+        table.wait()
     weights = []
     for slot in range(MB):
-        batch = order[slot, s]
+        batch = order_table[slot, s]
         weight = jnp.float32(0.0)
         for m in range(MB):
-            weight = weight + jnp.where(batch == m, micro_weight[m, r], 0.0)
+            weight = weight + jnp.where(batch == m, weight_table[m, r], 0.0)
         weights.append(weight)
 
     row_at = lax.broadcasted_iota(jnp.int32, (BLK, BLK), 0)
@@ -149,20 +193,25 @@
         return square, diagonal
 
     def compute(chunk):
+        group = [g for g in range(len(GROUPS)) if chunk in GROUPS[g]][0]
+        size, at = len(GROUPS[group]), GROUPS[group].index(chunk)
         for half in range(2):
             for i in range(SIDE):
                 square, diagonal = unit(half, y_orders[half][i], z_orders[half][chunk])
-                top, bottom = square[:TOP], square[TOP:]
                 if i < 2:
-                    give[half, chunk, i * TOP:(i + 1) * TOP, :] = top
-                    if i == 0:
-                        give[half, chunk, 2 * TOP:, :] = jnp.broadcast_to(diagonal, (8, BLK))
-                    else:
-                        give[half, chunk, 2 * TOP + 1:2 * TOP + 2, :] = diagonal
+                    words, marks = encode(square, diagonal, row_at, col_at)
+                    row = GIVE_AT[group] + (i * size + at) * CODED
+                    give[half, row:row + CODED, :] = words
+                    row = GIVE_AT[group] + 2 * size * CODED + 3 * (i * size + at)
+                    for mark in marks:
+                        give[half, row:row + 1, :] = mark
+                        row += 1
+                elif i == 2:
+                    pass_on[half, chunk, :BLK, :] = square
+                    pass_on[half, chunk, BLK:, :] = jnp.broadcast_to(diagonal, (8, BLK))
                 else:
-                    keep[half, chunk, i - 2, :TOP, :] = top
-                    keep[half, chunk, i - 2, TOP:, :] = jnp.broadcast_to(diagonal, (8, BLK))
-                (low_give if chunk < 2 else low_keep)[half, i, chunk % 2] = bottom
+                    keep[half, chunk, :BLK, :] = square
+                    keep[half, chunk, BLK:, :] = jnp.broadcast_to(diagonal, (8, BLK))
 
     def remote(src, dst, send, recv, to):
         return pltpu.make_async_remote_copy(
@@ -175,158 +224,133 @@
     z_first = [flip1(z), flip3(z)]
     z_second = [flip3(z), flip1(z)]
     to_s, to_y = final_target(s, y)
-    halves, chunks = range(2), range(SIDE)
-
-    step_y1 = [[remote(give.at[h, c], got_y1.at[h, c], y1_send.at[h, c], y1_recv.at[h, c],
-                       (s, y_first[h], z)) for c in chunks] for h in halves]
-    step_y2 = [[remote(keep.at[h, c, 0], got_y2.at[h, c], y2_send.at[h, c], y2_recv.at[h, c],
-                       (s, y_second[h], z)) for c in chunks] for h in halves]
-    step_z1 = [remote(keep.at[h, 0, 1], got_z1.at[h], z1_send.at[h], z1_recv.at[h],
+    halves, chunks, groups = range(2), range(SIDE), range(len(GROUPS))
+
+    def give_part(ref, h, g):
+        return ref.at[h, pl.ds(GIVE_AT[g], GIVE_AT[g + 1] - GIVE_AT[g])]
+
+    def pass_part(ref, h, g):
+        return ref.at[h, pl.ds(PASS_AT[g], PASS_AT[g + 1] - PASS_AT[g])]
+
+    step_y1 = [[remote(give_part(give, h, g), give_part(got_y1, h, g), y1_send.at[h, g],
+                       y1_recv.at[h, g], (s, y_first[h], z)) for g in groups] for h in halves]
+    step_y2 = [[remote(pass_part(coded, h, g), pass_part(got_y2, h, g), y2_send.at[h, g],
+                       y2_recv.at[h, g], (s, y_second[h], z)) for g in groups] for h in halves]
+    step_z1 = [remote(keep.at[h, 0], got_z1.at[h], z1_send.at[h], z1_recv.at[h],
                       (s, y, z_first[h])) for h in halves]
-    step_f = [[remote(keep.at[h, 1 + j, 1], got_f.at[h, j], f_send.at[h, j], f_recv.at[h, j],
+    step_f = [[remote(keep.at[h, 1 + j], got_f.at[h, j], f_send.at[h, j], f_recv.at[h, j],
                       (to_s, to_y, to_z))
                for j, to_z in enumerate((z_first[h], z_second[h], z))] for h in halves]
-    low_step_z1 = [[remote(low_give.at[h, i], low_z1.at[h, i], lz1_send.at[h, i],
-                           lz1_recv.at[h, i], (s, y, z_first[h])) for i in chunks] for h in halves]
-    low_step_y1 = [[remote(low_keep.at[h, i], low_y1.at[h, i], ly1_send.at[h, i],
-                           ly1_recv.at[h, i], (s, y_first[h], z)) for i in range(2)] for h in halves]
-    low_step_y2 = [remote(low_keep.at[h, 2], low_y2.at[h], ly2_send.at[h], ly2_recv.at[h],
-                          (s, y_second[h], z)) for h in halves]
-    low_step_f = [[remote(low_keep.at[h, 3, j], low_f.at[h, j], lf_send.at[h, j],
-                          lf_recv.at[h, j], (to_s, to_y, to_z))
-                   for j, to_z in enumerate((z_second[h], z))] for h in halves]
-
-    def add_first(h, c, i):
-        keep[h, c, i, :TOP] = keep[h, c, i, :TOP] + got_y1[h, c, i * TOP:(i + 1) * TOP]
-        at = 2 * TOP + i
-        keep[h, c, i, TOP:TOP + 1] = keep[h, c, i, TOP:TOP + 1] + got_y1[h, c, at:at + 1]
-
-    def after_y1(c):
+    def start_y1(g):
         for h in halves:
-            step_y1[h][c].wait_recv()
-            add_first(h, c, 0)
-            step_y2[h][c].start()
-            if c + 2 < SIDE:
-                step_y1[h][c + 2].start()
-            add_first(h, c, 1)
-
-    def after_y2(c):
+            step_y1[h][g].start()
+
+    def add_coded(ref, h, c, got, words_at, marks_at):
+        words = got[h, words_at:words_at + CODED]
+        marks = [got[h, marks_at + i:marks_at + i + 1] for i in range(3)]
+        square, diagonal = decode(words, marks, row_at, col_at)
+        ref[h, c, :BLK] = ref[h, c, :BLK] + square
+        ref[h, c, BLK:BLK + 1] = ref[h, c, BLK:BLK + 1] + diagonal
+
+    def after_y1(g):
+        size, base, mine = len(GROUPS[g]), GIVE_AT[g], PASS_AT[g]
+        marks = base + 2 * size * CODED
         for h in halves:
-            step_y2[h][c].wait_recv()
-            if c == 2:
-                step_z1[h].wait_recv()
-                keep[h, c, 1] = keep[h, c, 1] + (got_y2[h, c] + got_z1[h])
-            else:
-                keep[h, c, 1] = keep[h, c, 1] + got_y2[h, c]
-            (step_z1[h] if c == 0 else step_f[h][c - 1]).start()
-
-    def after_low_z1(i):
+            step_y1[h][g].wait_recv()
+            for at in range(size):
+                c = GROUPS[g][at]
+                add_coded(pass_on, h, c, got_y1, base + at * CODED, marks + 3 * at)
+                words, extra = encode(
+                    pass_on[h, c, :BLK], pass_on[h, c, BLK:BLK + 1], row_at, col_at
+                )
+                row = mine + at * CODED
+                coded[h, row:row + CODED] = words
+                row = mine + size * CODED + 3 * at
+                for mark in extra:
+                    coded[h, row:row + 1] = mark
+                    row += 1
+            step_y2[h][g].start()
         for h in halves:
-            low_step_z1[h][i].wait_recv()
-            low_keep[h, i] = low_keep[h, i] + low_z1[h, i]
-            if i < 2:
-                low_step_y1[h][i].start()
-
-    def after_low_y1():
+            for at in range(size):
+                c, place = GROUPS[g][at], size + at
+                add_coded(keep, h, c, got_y1, base + place * CODED, marks + 3 * place)
+
+    def after_y2(g):
+        size = len(GROUPS[g])
         for h in halves:
-            for i in range(2):
-                low_step_y1[h][i].wait_recv()
-                low_keep[h, 2 + i] = low_keep[h, 2 + i] + low_y1[h, i]
-                if i == 0:
-                    low_step_y2[h].start()
-
-    def after_low_y2():
-        for h in halves:
-            low_step_y2[h].wait_recv()
-            low_keep[h, 3] = low_keep[h, 3] + low_y2[h]
-            for j in range(2):
-                low_step_f[h][j].start()
+            step_y2[h][g].wait_recv()
+            for at in range(size):
+                c, base = GROUPS[g][at], PASS_AT[g]
+                add_coded(keep, h, c, got_y2, base + at * CODED, base + size * CODED + 3 * at)
+                if c == 2:
+                    step_z1[h].wait_recv()
+                    keep[h, c] = keep[h, c] + got_z1[h]
+                (step_z1[h] if c == 0 else step_f[h][c - 1]).start()
 
     fetched(0)
     compute(0)
     pl.semaphore_wait(barrier, len(greet))
-    for h in halves:
-        step_y1[h][0].start()
+    start_y1(0)
     fetched(1)
-    fetched(2)
     compute(1)
-    for h in halves:
-        step_y1[h][1].start()
-        for i in chunks:
-            low_step_z1[h][i].start()
+    start_y1(1)
     compute(2)
-    fetched(3)
     compute(3)
     after_y1(0)
-    after_low_z1(0)
-    after_low_z1(1)
+    start_y1(2)
     after_y1(1)
+    start_y1(3)
     after_y2(0)
-    after_low_z1(2)
-    after_low_z1(3)
     after_y1(2)
-    after_low_y1()
     after_y2(1)
     after_y1(3)
-    after_low_y2()
     after_y2(2)
     after_y2(3)
+    weight_sum = jnp.float32(0.0)
+    for m in range(MB):
+        for other in range(REPLICAS):
+            weight_sum = weight_sum + weight_table[m, other]
+    shrink = 1.0 / (MROWS * jnp.full((8, BLK), weight_sum))[:1]
     for h in halves:
-        for c in chunks:
-            step_y1[h][c].wait_send()
-            step_y2[h][c].wait_send()
-            low_step_z1[h][c].wait_send()
+        for g in groups:
+            step_y1[h][g].wait_send()
+            step_y2[h][g].wait_send()
         step_z1[h].wait_send()
-        low_step_y1[h][0].wait_send()
-        low_step_y1[h][1].wait_send()
-        low_step_y2[h].wait_send()
-    for h in halves:
-        for j in range(2):
-            low_step_f[h][j].wait_recv()
-        out[h, TOP:BLK] = low_f[h, 0] + low_f[h, 1]
     for h in halves:
         for j in range(3):
             step_f[h][j].wait_recv()
-        total = got_f[h, 0] + got_f[h, 1] + got_f[h, 2]
-        out[h, :TOP] = total[:TOP]
-        out[h, BLK:] = total[TOP:]
+        out[h] = (got_f[h, 0] + got_f[h, 1] + got_f[h, 2]) * shrink
     for h in halves:
         for j in range(3):
             step_f[h][j].wait_send()
-        for j in range(2):
-            low_step_f[h][j].wait_send()
 
 
 def reduce_blocks(sent_act, sent_grad, embedded, loss_grad, micro_weight, order):
     dma = pltpu.SemaphoreType.DMA
-    block = (TOP + 8, BLK)
-    pair = (2 * TOP + 8, BLK)
-    low = (2, LOW, BLK)
-    hbm, smem = pl.BlockSpec(memory_space=pltpu.HBM), pl.BlockSpec(memory_space=pltpu.SMEM)
+    block = (PACKED, BLK)
+    given, passed = (2, GIVE_AT[-1], BLK), (2, PASS_AT[-1], BLK)
+    count = len(GROUPS)
+    hbm = pl.BlockSpec(memory_space=pltpu.HBM)
     return pl.pallas_call(
         reduce_kernel,
         out_shape=jax.ShapeDtypeStruct((2, PACKED, BLK), jnp.float32),
-        in_specs=[hbm] * 4 + [smem] * 2,
+        in_specs=[hbm] * 6,
         out_specs=pl.BlockSpec(memory_space=pltpu.VMEM),
         scratch_shapes=[
             pltpu.VMEM((ROWS, 2 * D), jnp.bfloat16),
-            pltpu.VMEM((2, SIDE) + pair, jnp.float32),
-            pltpu.VMEM((2, SIDE, 2) + block, jnp.float32),
-            pltpu.VMEM((2, SIDE) + pair, jnp.float32),
+            pltpu.VMEM(given, jnp.int32),
             pltpu.VMEM((2, SIDE) + block, jnp.float32),
+            pltpu.VMEM(passed, jnp.int32),
+            pltpu.VMEM((2, SIDE) + block, jnp.float32),
+            pltpu.VMEM(given, jnp.int32),
+            pltpu.VMEM(passed, jnp.int32),
             pltpu.VMEM((2,) + block, jnp.float32),
             pltpu.VMEM((2, 3) + block, jnp.float32),
-            pltpu.VMEM((2, SIDE) + low, jnp.float32),
-            pltpu.VMEM((2, SIDE) + low, jnp.float32),
-            pltpu.VMEM((2, SIDE) + low, jnp.float32),
-            pltpu.VMEM((2, 2) + low, jnp.float32),
-            pltpu.VMEM((2,) + low, jnp.float32),
-            pltpu.VMEM((2,) + low, jnp.float32),
-            dma((SIDE, SIDE)),
-            dma((2, SIDE)), dma((2, SIDE)), dma((2, SIDE)), dma((2, SIDE)),
+            pltpu.SMEM((MB, REPLICAS), jnp.float32),
+            pltpu.SMEM((MB, SECTIONS), jnp.int32),
+            dma((2, SIDE)), dma((2,)),
+            dma((2, count)), dma((2, count)), dma((2, count)), dma((2, count)),
             dma((2,)), dma((2,)), dma((2, 3)), dma((2, 3)),
-            dma((2, SIDE)), dma((2, SIDE)), dma((2, 2)), dma((2, 2)),
-            dma((2,)), dma((2,)), dma((2, 2)), dma((2, 2)),
         ],
         compiler_params=pltpu.CompilerParams(
             collective_id=0, has_side_effects=True, vmem_limit_bytes=VMEM_LIMIT
@@ -404,7 +428,7 @@
             work[m, start:start + PANEL, :] = swept
 
 
-def invert_kernel(micro_weight, assignment, packed, old_hbm, out_hbm, work, old, out, mask, sems):
+def invert_kernel(assignment, packed, old_hbm, out_hbm, work, old, out, mask, sems):
     r = lax.axis_index("dp")
     get_old = pltpu.make_async_copy(old_hbm, old, sems.at[0])
     get_mask = pltpu.make_async_copy(assignment, mask, sems.at[1])
@@ -414,15 +438,14 @@
     col_at = lax.broadcasted_iota(jnp.int32, (BLK, BLK), 1)
     on_diagonal = row_at == col_at
     identity = jnp.where(on_diagonal, 1.0, 0.0)
-    scale = 1.0 / (MROWS * total(micro_weight[...]))
     for half in range(2):
         square = packed[half, :BLK, :]
         flipped = square.T
         one = jnp.where(row_at >= col_at, square, flipped)
         two = jnp.where(row_at < col_at, square, flipped)
         two = jnp.where(on_diagonal, packed[half, BLK:BLK + 1, :], two)
-        work[2 * half] = one * scale + damping * identity
-        work[2 * half + 1] = two * scale + damping * identity
+        work[2 * half] = one + damping * identity
+        work[2 * half + 1] = two + damping * identity
 
     every = range(OWN)
     factors = [work[m] for m in every]
@@ -471,12 +494,12 @@
         put.wait()
 
 
-def invert_blocks(micro_weight, assignment, packed, old_inverse):
+def invert_blocks(assignment, packed, old_inverse):
     vmem, hbm = pl.BlockSpec(memory_space=pltpu.VMEM), pl.BlockSpec(memory_space=pltpu.HBM)
     return pl.pallas_call(
         invert_kernel,
         out_shape=jax.ShapeDtypeStruct(old_inverse.shape, jnp.float32),
-        in_specs=[vmem, hbm, vmem, hbm],
+        in_specs=[hbm, vmem, hbm],
         out_specs=hbm,
         scratch_shapes=[
             pltpu.VMEM((OWN, BLK, BLK), jnp.float32),
@@ -487,13 +510,12 @@
         ],
         compiler_params=pltpu.CompilerParams(vmem_limit_bytes=VMEM_LIMIT),
         name="invert",
-    )(micro_weight, assignment, packed, old_inverse)
+    )(assignment, packed, old_inverse)
 
 
 def shards(sent_act, sent_grad, embedded, loss_grad, micro_weight, order, assignment, old_inverse):
-    micro_weight = micro_weight.T
-    packed = reduce_blocks(sent_act, sent_grad, embedded, loss_grad, micro_weight, order.T)
-    return invert_blocks(micro_weight, assignment, packed, old_inverse)
+    packed = reduce_blocks(sent_act, sent_grad, embedded, loss_grad, micro_weight.T, order.T)
+    return invert_blocks(assignment, packed, old_inverse)
 
 
 def solution(mesh):

time: 44.3 us -> 42.7 us (0.964)
  the two profiles are of different devices: /device:TPU:1 before, /device:TPU:31 now
where the time goes in v4:
time: 42.7 us; the launch traced here: 42.6 us
  Pallas kernels  42.6 us (100%)
    pallas_call x1, Pallas kernels, reduce_blocks(): pl.pallas_call(reduce_kernel, out_shape=jax.ShapeDtypeStruct((2, PACKED,...  33 us
    pallas_call x1, Pallas kernels, invert_blocks(): pl.pallas_call(invert_kernel, out_shape=jax.ShapeDtypeStruct(old_inverse....  9.63 us

profile of v4, /device:TPU:31, one launch (start us, length us, event | category | flops | bytes accessed | tf_op | source)
XLA Modules:
  0.0 42.6 jit_solution(3812777363823523110)
XLA Ops:
  0.0 33.0 %gram_reduce.1.packed = f32[2,136,128]{2,1,0:T(8,128)} custom-call(bf16[1,256,4096]{2,1,0:T(8,128)(2,1)} %sent_act.1, bf16[1,256,4096]{2,1,0:T(8,128)(2,1)} %sent_grad.1, bf16[256,4096]{1,0:T(8,128)(2,1)} %embedded.1, bf16[256,4096]{1,0:T(8,128)(2,1)} %loss_grad.1, f32[4,16]{1,0:T(4,128)} %bitcast.2, s32[4,16]{1,0:T(4,128)} %bitcast.3), custom_call_target="tpu_custom_call" | custom-call | tf_op jit(solution)/shard_map/gram_reduce/pallas_call | solution.py:334
  33.0 9.6 %invert.1 = f32[1,4,128,128]{3,2,1,0:T(8,128)} custom-call(s32[1,64]{1,0:T(1,128)} %assignment.1, f32[2,136,128]{2,1,0:T(8,128)} %gram_reduce.1.packed, f32[1,4,128,128]{3,2,1,0:T(8,128)} %old_hbm.1), custom_call_target="tpu_custom_call" | custom-call | tf_op jit(solution)/shard_map/invert/pallas_call | solution.py:499

commit v5 on v4

--- a/solution.py
+++ b/solution.py
@@ -19,15 +19,6 @@
 QUARTER = BLK // 4
 CODED = 3 * QUARTER
 BITS = 22.0
-GROUPS = ((0,), (1,), (2,), (3,))
-
-
-def message_rows(units):
-    return units * CODED + -(-3 * units // 8) * 8
-
-
-GIVE_AT = [sum(message_rows(2 * len(g)) for g in GROUPS[:i]) for i in range(len(GROUPS) + 1)]
-PASS_AT = [sum(message_rows(len(g)) for g in GROUPS[:i]) for i in range(len(GROUPS) + 1)]
 PANEL = 8
 ROUNDS = 2
 LIMIT = 1e-6
@@ -124,7 +115,7 @@
         wide = pl.ds(pl.multiple_of(column, 2 * OWN * BLK), 2 * OWN * BLK)
         narrow = pl.ds(pl.multiple_of(column - to_y // 2 * D, 2 * OWN * BLK), 2 * OWN * BLK)
         return pltpu.make_async_copy(
-            src.at[:, narrow], rows.at[:, wide], in_sem.at[place, to_y]
+            src.at[:, narrow], rows.at[:, wide], in_sem.at[place]
         )
 
     for place in range(2):
@@ -153,8 +144,7 @@
                 table.start()
 
     def fetched(place):
-        for to_y in range(SIDE):
-            fetch(sent_act.at[0], to_y, place).wait()
+        pltpu.make_async_copy(sent_act.at[0], rows.at[:, pl.ds(0, D)], in_sem.at[place]).wait()
 
     for table in tables:
         table.wait()
@@ -192,26 +182,24 @@
         diagonal = jnp.sum(jnp.where(row_at == col_at, second, 0.0), axis=0, keepdims=True)
         return square, diagonal
 
-    def compute(chunk):
-        group = [g for g in range(len(GROUPS)) if chunk in GROUPS[g]][0]
-        size, at = len(GROUPS[group]), GROUPS[group].index(chunk)
+    def put(place, words, marks):
+        place[:CODED, :] = words
+        for i, mark in enumerate(marks):
+            place[CODED + i:CODED + i + 1, :] = mark
+
+    def compute_give(chunk):
         for half in range(2):
-            for i in range(SIDE):
+            for i in range(2):
                 square, diagonal = unit(half, y_orders[half][i], z_orders[half][chunk])
-                if i < 2:
-                    words, marks = encode(square, diagonal, row_at, col_at)
-                    row = GIVE_AT[group] + (i * size + at) * CODED
-                    give[half, row:row + CODED, :] = words
-                    row = GIVE_AT[group] + 2 * size * CODED + 3 * (i * size + at)
-                    for mark in marks:
-                        give[half, row:row + 1, :] = mark
-                        row += 1
-                elif i == 2:
-                    pass_on[half, chunk, :BLK, :] = square
-                    pass_on[half, chunk, BLK:, :] = jnp.broadcast_to(diagonal, (8, BLK))
-                else:
-                    keep[half, chunk, :BLK, :] = square
-                    keep[half, chunk, BLK:, :] = jnp.broadcast_to(diagonal, (8, BLK))
+                words, marks = encode(square, diagonal, row_at, col_at)
+                put(give.at[half, i, chunk], words, marks)
+
+    def compute_keep(chunk):
+        for half in range(2):
+            for i, ref in enumerate((pass_on, keep)):
+                square, diagonal = unit(half, y_orders[half][2 + i], z_orders[half][chunk])
+                ref[half, chunk, :BLK, :] = square
+                ref[half, chunk, BLK:, :] = jnp.broadcast_to(diagonal, (8, BLK))
 
     def remote(src, dst, send, recv, to):
         return pltpu.make_async_remote_copy(
@@ -224,112 +212,98 @@
     z_first = [flip1(z), flip3(z)]
     z_second = [flip3(z), flip1(z)]
     to_s, to_y = final_target(s, y)
-    halves, chunks, groups = range(2), range(SIDE), range(len(GROUPS))
-
-    def give_part(ref, h, g):
-        return ref.at[h, pl.ds(GIVE_AT[g], GIVE_AT[g + 1] - GIVE_AT[g])]
-
-    def pass_part(ref, h, g):
-        return ref.at[h, pl.ds(PASS_AT[g], PASS_AT[g + 1] - PASS_AT[g])]
-
-    step_y1 = [[remote(give_part(give, h, g), give_part(got_y1, h, g), y1_send.at[h, g],
-                       y1_recv.at[h, g], (s, y_first[h], z)) for g in groups] for h in halves]
-    step_y2 = [[remote(pass_part(coded, h, g), pass_part(got_y2, h, g), y2_send.at[h, g],
-                       y2_recv.at[h, g], (s, y_second[h], z)) for g in groups] for h in halves]
-    step_z1 = [remote(keep.at[h, 0], got_z1.at[h], z1_send.at[h], z1_recv.at[h],
+    halves, chunks = range(2), range(SIDE)
+
+    step_y1 = [[[remote(give.at[h, i, c], got_y1.at[h, i, c], y1_send, y1_recv.at[h, i, c],
+                        (s, y_first[h], z)) for c in chunks] for i in range(2)] for h in halves]
+    step_y2 = [[remote(coded.at[h, c], got_y2.at[h, c], y2_send, y2_recv.at[h, c],
+                       (s, y_second[h], z)) for c in chunks] for h in halves]
+    step_z1 = [remote(keep.at[h, 0], got_z1.at[h], z1_send, z1_recv.at[h],
                       (s, y, z_first[h])) for h in halves]
-    step_f = [[remote(keep.at[h, 1 + j], got_f.at[h, j], f_send.at[h, j], f_recv.at[h, j],
+    step_f = [[remote(keep.at[h, 1 + j], got_f.at[h, j], f_send, f_recv.at[h],
                       (to_s, to_y, to_z))
                for j, to_z in enumerate((z_first[h], z_second[h], z))] for h in halves]
-    def start_y1(g):
+    def start_y1(i, c):
         for h in halves:
-            step_y1[h][g].start()
-
-    def add_coded(ref, h, c, got, words_at, marks_at):
-        words = got[h, words_at:words_at + CODED]
-        marks = [got[h, marks_at + i:marks_at + i + 1] for i in range(3)]
-        square, diagonal = decode(words, marks, row_at, col_at)
-        ref[h, c, :BLK] = ref[h, c, :BLK] + square
-        ref[h, c, BLK:BLK + 1] = ref[h, c, BLK:BLK + 1] + diagonal
-
-    def after_y1(g):
-        size, base, mine = len(GROUPS[g]), GIVE_AT[g], PASS_AT[g]
-        marks = base + 2 * size * CODED
+            step_y1[h][i][c].start()
+
+    def unpack(place):
+        marks = [place[CODED + i:CODED + i + 1] for i in range(3)]
+        return decode(place[:CODED], marks, row_at, col_at)
+
+    def after_y1(c):
         for h in halves:
-            step_y1[h][g].wait_recv()
-            for at in range(size):
-                c = GROUPS[g][at]
-                add_coded(pass_on, h, c, got_y1, base + at * CODED, marks + 3 * at)
-                words, extra = encode(
-                    pass_on[h, c, :BLK], pass_on[h, c, BLK:BLK + 1], row_at, col_at
-                )
-                row = mine + at * CODED
-                coded[h, row:row + CODED] = words
-                row = mine + size * CODED + 3 * at
-                for mark in extra:
-                    coded[h, row:row + 1] = mark
-                    row += 1
-            step_y2[h][g].start()
+            step_y1[h][0][c].wait_recv()
+            square, diagonal = unpack(got_y1.at[h, 0, c])
+            words, marks = encode(
+                pass_on[h, c, :BLK] + square, pass_on[h, c, BLK:BLK + 1] + diagonal,
+                row_at, col_at,
+            )
+            put(coded.at[h, c], words, marks)
+            step_y2[h][c].start()
+
+    def finish(c):
         for h in halves:
-            for at in range(size):
-                c, place = GROUPS[g][at], size + at
-                add_coded(keep, h, c, got_y1, base + place * CODED, marks + 3 * place)
-
-    def after_y2(g):
-        size = len(GROUPS[g])
-        for h in halves:
-            step_y2[h][g].wait_recv()
-            for at in range(size):
-                c, base = GROUPS[g][at], PASS_AT[g]
-                add_coded(keep, h, c, got_y2, base + at * CODED, base + size * CODED + 3 * at)
-                if c == 2:
-                    step_z1[h].wait_recv()
-                    keep[h, c] = keep[h, c] + got_z1[h]
-                (step_z1[h] if c == 0 else step_f[h][c - 1]).start()
+            step_y1[h][1][c].wait_recv()
+            square, diagonal = unpack(got_y1.at[h, 1, c])
+            square, diagonal = keep[h, c, :BLK] + square, keep[h, c, BLK:BLK + 1] + diagonal
+            step_y2[h][c].wait_recv()
+            more, extra = unpack(got_y2.at[h, c])
+            square, diagonal = square + more, diagonal + extra
+            if c == 2:
+                step_z1[h].wait_recv()
+                square = square + got_z1[h, :BLK]
+                diagonal = diagonal + got_z1[h, BLK:BLK + 1]
+            keep[h, c, :BLK] = square
+            keep[h, c, BLK:BLK + 1] = diagonal
+            (step_z1[h] if c == 0 else step_f[h][c - 1]).start()
 
     fetched(0)
-    compute(0)
+    compute_give(0)
     pl.semaphore_wait(barrier, len(greet))
-    start_y1(0)
+    start_y1(0, 0)
     fetched(1)
-    compute(1)
-    start_y1(1)
-    compute(2)
-    compute(3)
+    compute_give(1)
+    start_y1(0, 1)
+    start_y1(1, 0)
+    compute_keep(0)
+    compute_give(2)
     after_y1(0)
-    start_y1(2)
+    start_y1(0, 2)
+    start_y1(1, 1)
+    compute_keep(1)
     after_y1(1)
-    start_y1(3)
-    after_y2(0)
+    compute_give(3)
+    start_y1(0, 3)
+    compute_keep(2)
+    finish(0)
+    start_y1(1, 2)
     after_y1(2)
-    after_y2(1)
+    compute_keep(3)
+    start_y1(1, 3)
+    finish(1)
     after_y1(3)
-    after_y2(2)
-    after_y2(3)
+    finish(2)
+    finish(3)
     weight_sum = jnp.float32(0.0)
     for m in range(MB):
         for other in range(REPLICAS):
             weight_sum = weight_sum + weight_table[m, other]
     shrink = 1.0 / (MROWS * jnp.full((8, BLK), weight_sum))[:1]
+    here = (s, y_first[0], z)
+    remote(give, got_y1, y1_send, z1_recv.at[0], here).wait_send()
+    remote(coded, got_y2, y2_send, z1_recv.at[0], here).wait_send()
+    remote(got_z1, got_z1, z1_send, z1_recv.at[0], here).wait_send()
     for h in halves:
-        for g in groups:
-            step_y1[h][g].wait_send()
-            step_y2[h][g].wait_send()
-        step_z1[h].wait_send()
-    for h in halves:
-        for j in range(3):
-            step_f[h][j].wait_recv()
+        remote(got_f.at[h], got_f.at[h], f_send, f_recv.at[h], here).wait_recv()
         out[h] = (got_f[h, 0] + got_f[h, 1] + got_f[h, 2]) * shrink
-    for h in halves:
-        for j in range(3):
-            step_f[h][j].wait_send()
+    remote(got_f, got_f, f_send, f_recv.at[0], here).wait_send()
 
 
 def reduce_blocks(sent_act, sent_grad, embedded, loss_grad, micro_weight, order):
     dma = pltpu.SemaphoreType.DMA
     block = (PACKED, BLK)
-    given, passed = (2, GIVE_AT[-1], BLK), (2, PASS_AT[-1], BLK)
-    count = len(GROUPS)
+    message = (CODED + 8, BLK)
     hbm = pl.BlockSpec(memory_space=pltpu.HBM)
     return pl.pallas_call(
         reduce_kernel,
@@ -338,19 +312,18 @@
         out_specs=pl.BlockSpec(memory_space=pltpu.VMEM),
         scratch_shapes=[
             pltpu.VMEM((ROWS, 2 * D), jnp.bfloat16),
-            pltpu.VMEM(given, jnp.int32),
+            pltpu.VMEM((2, 2, SIDE) + message, jnp.int32),
             pltpu.VMEM((2, SIDE) + block, jnp.float32),
-            pltpu.VMEM(passed, jnp.int32),
+            pltpu.VMEM((2, SIDE) + message, jnp.int32),
             pltpu.VMEM((2, SIDE) + block, jnp.float32),
-            pltpu.VMEM(given, jnp.int32),
-            pltpu.VMEM(passed, jnp.int32),
+            pltpu.VMEM((2, 2, SIDE) + message, jnp.int32),
+            pltpu.VMEM((2, SIDE) + message, jnp.int32),
             pltpu.VMEM((2,) + block, jnp.float32),
             pltpu.VMEM((2, 3) + block, jnp.float32),
             pltpu.SMEM((MB, REPLICAS), jnp.float32),
             pltpu.SMEM((MB, SECTIONS), jnp.int32),
-            dma((2, SIDE)), dma((2,)),
-            dma((2, count)), dma((2, count)), dma((2, count)), dma((2, count)),
-            dma((2,)), dma((2,)), dma((2, 3)), dma((2, 3)),
+            dma((2,)), dma((2,)),
+            dma, dma((2, 2, SIDE)), dma, dma((2, SIDE)), dma, dma((2,)), dma, dma((2,)),
         ],
         compiler_params=pltpu.CompilerParams(
             collective_id=0, has_side_effects=True, vmem_limit_bytes=VMEM_LIMIT

time: 42.7 us -> 40.4 us (0.946)
  the two profiles are of different devices: /device:TPU:31 before, /device:TPU:1 now
where the time goes in v5:
time: 40.4 us; the launch traced here: 40.3 us
  Pallas kernels  40.3 us (100%)
    pallas_call x1, Pallas kernels, reduce_blocks(): pl.pallas_call(reduce_kernel, out_shape=jax.ShapeDtypeStruct((2, PACKED,...  30.6 us
    pallas_call x1, Pallas kernels, invert_blocks(): pl.pallas_call(invert_kernel, out_shape=jax.ShapeDtypeStruct(old_inverse....  9.64 us

profile of v5, /device:TPU:1, one launch (start us, length us, event | category | flops | bytes accessed | tf_op | source)
XLA Modules:
  0.0 40.3 jit_solution(12536219214480285015)
XLA Ops:
  0.0 30.6 %gram_reduce.1.packed = f32[2,136,128]{2,1,0:T(8,128)} custom-call(bf16[1,256,4096]{2,1,0:T(8,128)(2,1)} %sent_act.1, bf16[1,256,4096]{2,1,0:T(8,128)(2,1)} %sent_grad.1, bf16[256,4096]{1,0:T(8,128)(2,1)} %embedded.1, bf16[256,4096]{1,0:T(8,128)(2,1)} %loss_grad.1, f32[4,16]{1,0:T(4,128)} %bitcast.2, s32[4,16]{1,0:T(4,128)} %bitcast.3), custom_call_target="tpu_custom_call" | custom-call | tf_op jit(solution)/shard_map/gram_reduce/pallas_call | solution.py:308
  30.6 9.6 %invert.1 = f32[1,4,128,128]{3,2,1,0:T(8,128)} custom-call(s32[1,64]{1,0:T(1,128)} %assignment.1, f32[2,136,128]{2,1,0:T(8,128)} %gram_reduce.1.packed, f32[1,4,128,128]{3,2,1,0:T(8,128)} %old_hbm.1), custom_call_target="tpu_custom_call" | custom-call | tf_op jit(solution)/shard_map/invert/pallas_call | solution.py:472

commit v6 on v5

--- a/solution.py
+++ b/solution.py
@@ -15,7 +15,7 @@
 SIDE = 4
 SECTIONS = 16
 REPLICAS = 16
-PACKED = BLK + 8
+PACKED = BLK + 1
 QUARTER = BLK // 4
 CODED = 3 * QUARTER
 BITS = 22.0
@@ -110,15 +110,18 @@
     ]
 
     def fetch(src, to_y, place):
-        pair = (z // 2 + 1 + place) % 2
-        column = (to_y * SIDE + pair * 2) * OWN * BLK
-        wide = pl.ds(pl.multiple_of(column, 2 * OWN * BLK), 2 * OWN * BLK)
-        narrow = pl.ds(pl.multiple_of(column - to_y // 2 * D, 2 * OWN * BLK), 2 * OWN * BLK)
+        first = (to_y * SIDE + flip2(z)) * OWN * BLK
+        second = (to_y * SIDE + z // 2 * 2) * OWN * BLK
+        third = (to_y * SIDE + z // 2 * -2 + 2 + (z + 1) % 2) * OWN * BLK
+        column = (first, second, third)[place]
+        size = (OWN, 2 * OWN, OWN)[place] * BLK
+        wide = pl.ds(pl.multiple_of(column, size), size)
+        narrow = pl.ds(pl.multiple_of(column - to_y // 2 * D, size), size)
         return pltpu.make_async_copy(
             src.at[:, narrow], rows.at[:, wide], in_sem.at[place]
         )
 
-    for place in range(2):
+    for place in range(3):
         @pl.when(s < SECTIONS - 1)
         def _():
             for to_y in range(2):
@@ -144,7 +147,10 @@
                 table.start()
 
     def fetched(place):
-        pltpu.make_async_copy(sent_act.at[0], rows.at[:, pl.ds(0, D)], in_sem.at[place]).wait()
+        size = (4, 8, 4)[place] * OWN * BLK
+        pltpu.make_async_copy(
+            sent_act.at[0, :, pl.ds(0, size)], rows.at[:, pl.ds(0, size)], in_sem.at[place]
+        ).wait()
 
     for table in tables:
         table.wait()
@@ -199,7 +205,7 @@
             for i, ref in enumerate((pass_on, keep)):
                 square, diagonal = unit(half, y_orders[half][2 + i], z_orders[half][chunk])
                 ref[half, chunk, :BLK, :] = square
-                ref[half, chunk, BLK:, :] = jnp.broadcast_to(diagonal, (8, BLK))
+                ref[half, chunk, BLK:, :] = diagonal
 
     def remote(src, dst, send, recv, to):
         return pltpu.make_async_remote_copy(
@@ -263,24 +269,25 @@
     pl.semaphore_wait(barrier, len(greet))
     start_y1(0, 0)
     fetched(1)
+    fetched(2)
     compute_give(1)
     start_y1(0, 1)
     start_y1(1, 0)
+    compute_give(2)
     compute_keep(0)
-    compute_give(2)
     after_y1(0)
     start_y1(0, 2)
     start_y1(1, 1)
+    compute_give(3)
     compute_keep(1)
     after_y1(1)
-    compute_give(3)
     start_y1(0, 3)
+    start_y1(1, 2)
+    finish(0)
     compute_keep(2)
-    finish(0)
-    start_y1(1, 2)
     after_y1(2)
+    start_y1(1, 3)
     compute_keep(3)
-    start_y1(1, 3)
     finish(1)
     after_y1(3)
     finish(2)
@@ -303,7 +310,7 @@
 def reduce_blocks(sent_act, sent_grad, embedded, loss_grad, micro_weight, order):
     dma = pltpu.SemaphoreType.DMA
     block = (PACKED, BLK)
-    message = (CODED + 8, BLK)
+    message = (CODED + 3, BLK)
     hbm = pl.BlockSpec(memory_space=pltpu.HBM)
     return pl.pallas_call(
         reduce_kernel,
@@ -322,7 +329,7 @@
             pltpu.VMEM((2, 3) + block, jnp.float32),
             pltpu.SMEM((MB, REPLICAS), jnp.float32),
             pltpu.SMEM((MB, SECTIONS), jnp.int32),
-            dma((2,)), dma((2,)),
+            dma((3,)), dma((2,)),
             dma, dma((2, 2, SIDE)), dma, dma((2, SIDE)), dma, dma((2,)), dma, dma((2,)),
         ],
         compiler_params=pltpu.CompilerParams(

time: 40.4 us -> 39.7 us (0.983)
  Pallas kernels: 40.3 us -> 39.6 us
    pallas_call x1, Pallas kernels: 30.6 us -> 29.9 us  [reduce_blocks(): pl.pallas_call(reduce_kernel, out_shape=jax.ShapeDtypeStruct((2, PACKED,...]
where the time goes in v6:
time: 39.7 us; the launch traced here: 39.6 us
  Pallas kernels  39.6 us (100%)
    pallas_call x1, Pallas kernels, reduce_blocks(): pl.pallas_call(reduce_kernel, out_shape=jax.ShapeDtypeStruct((2, PACKED,...  29.9 us
    pallas_call x1, Pallas kernels, invert_blocks(): pl.pallas_call(invert_kernel, out_shape=jax.ShapeDtypeStruct(old_inverse....  9.64 us

profile of v6, /device:TPU:1, one launch (start us, length us, event | category | flops | bytes accessed | tf_op | source)
XLA Modules:
  0.0 39.6 jit_solution(13639879462964146749)
XLA Ops:
  0.0 29.9 %gram_reduce.1.packed = f32[2,129,128]{2,1,0:T(8,128)} custom-call(bf16[1,256,4096]{2,1,0:T(8,128)(2,1)} %sent_act.1, bf16[1,256,4096]{2,1,0:T(8,128)(2,1)} %sent_grad.1, bf16[256,4096]{1,0:T(8,128)(2,1)} %embedded.1, bf16[256,4096]{1,0:T(8,128)(2,1)} %loss_grad.1, f32[4,16]{1,0:T(4,128)} %bitcast.2, s32[4,16]{1,0:T(4,128)} %bitcast.3), custom_call_target="tpu_custom_call" | custom-call | tf_op jit(solution)/shard_map/gram_reduce/pallas_call | solution.py:315
  29.9 9.6 %invert.1 = f32[1,4,128,128]{3,2,1,0:T(8,128)} custom-call(s32[1,64]{1,0:T(1,128)} %assignment.1, f32[2,129,128]{2,1,0:T(8,128)} %gram_reduce.1.packed, f32[1,4,128,128]{3,2,1,0:T(8,128)} %old_hbm.1), custom_call_target="tpu_custom_call" | custom-call | tf_op jit(solution)/shard_map/invert/pallas_call | solution.py:479
